TPU v7x, 32 devices: a whole 2x2x4 slice. The times are simulated.
32 devices in a mesh: groups: 2 (over x), seg: 16 (over z, y, core).
Axes of the slice: x: 2, y: 2, z: 4, core: 2. Of those that a mesh axis runs over, the one named last changes fastest.
Arguments:
- bins: bfloat16 [1024, 128], P(('groups', 'seg')), parts along dimension 0, may hold values from -6 to 6
- conv_weight: bfloat16 [3, 128, 128], replicated, may hold values from -0.3125 to 0.3125
- conv_bias: float32 [128], replicated, may hold values from -3 to 3
- pair_left: bfloat16 [128, 48], replicated, may hold values from -0.5 to 0.5
- pair_right: bfloat16 [128, 48], replicated, may hold values from -0.5 to 0.5
- pair_weight: bfloat16 [3, 3, 48, 48], replicated, may hold values from -0.3125 to 0.3125
- pair_bias: float32 [48], replicated, may hold values from -3 to 3
- head: bfloat16 [48], replicated, may hold values from -0.875 to 0.875
- shifts: int32 [4], replicated, may hold values from -8 to 8, as said below
- flags: int32 [4], replicated, may hold values from 0 to 1, as said below
- dilations: int32 [2], replicated, may hold values from 1 to 4, as said below
Outputs:
- contacts: float32 [1024, 512], P(('groups', 'seg')), parts along dimension 0
There are 2 independent parts, one for each index of `groups`. A program takes and returns all parts, laid end to end along the dimension named above; an argument that names none is the same for every part. Nothing has to cross between parts.
Inputs may be any that keep to these rules, and one draw needn't show every extreme that they name: `shifts`: the largest entry is 8 and the smallest -8. `flags`: exactly half of the views are reverse-complemented. `dilations`: one of the two rates equals 4 and the other is smaller.
All inputs are finite; a program needn't handle non-finite values.
Results may differ from a plain program's by a relative error of at most 0.0055.
Values may be sent and summed in bfloat16 or wider, within the bound.
No kernel may reach another device: no remote copies, remote signals or barrier semaphores. Data moves between devices by JAX's collectives and lax.ppermute only.
A program may use at most 128 MiB of HBM per device.

v0:
```python
import jax
import jax.numpy as jnp
from jax import lax
from jax.sharding import PartitionSpec as P

CHANNELS = 128
PAIR_CH = 48
BAND = 512
VIEWS = 4
DMAX = 4
HALO = 12
AHEAD = 18


def extended(value, sides, width):
    for axis, dim in sides:
        size, length = (lax.axis_size(axis), value.shape[dim])
        up = [(i, (i + 1) % size) for i in range(size - 1)]
        down = [(j, i) for i, j in up]
        last = lax.slice_in_dim(value, length - width, length, axis=dim)
        leading = lax.slice_in_dim(value, 0, width, axis=dim)
        before = lax.ppermute(last, axis, up)
        after = lax.ppermute(leading, axis, down)
        value = jnp.concatenate([before, value, after], axis=dim)
    return value


def passed_along(block, axis, distance):
    devices = range(lax.axis_size(axis))
    route = [(i - distance, i) for i in devices if i - distance in devices]
    return lax.ppermute(block, axis, route)


def view_kernels(conv_weight, flags):
    flipped = conv_weight[::-1, ::-1, :]
    chosen = (flags == 1)[:, None, None, None]
    return jnp.where(chosen, flipped[None], conv_weight[None])


def trunk(source, base, rows, shifts, dilate_seq, kernels, conv_bias, pair_left, pair_right):

    def one_view(shift, kernel):
        start = base + shift
        taps = [
            lax.dynamic_slice_in_dim(source, start + (tap - 1) * dilate_seq, rows, 0)
            for tap in range(3)
        ]
        mixed = jnp.zeros((rows, CHANNELS), jnp.float32)
        for tap in range(3):
            mixed = mixed + jnp.dot(taps[tap], kernel[tap], preferred_element_type=jnp.float32)
        return (taps[1], mixed)

    centers, mixed = jax.vmap(one_view)(shifts, kernels)
    feature = (centers.astype(jnp.float32) + jax.nn.relu(mixed + conv_bias)).astype(jnp.bfloat16)
    left = jnp.einsum("vrc,cp->vrp", feature, pair_left, preferred_element_type=jnp.float32).astype(
        jnp.bfloat16
    )
    right = jnp.einsum(
        "vrc,cp->vrp", feature, pair_right, preferred_element_type=jnp.float32
    ).astype(jnp.bfloat16)
    return (left, right)


def pair_block(left_rows, right_rows, first_row, total, dilate_pair, pair_weight, pair_bias, head):
    span = left_rows.shape[1]
    rows_out = span - 2 * DMAX
    width = right_rows.shape[1]
    global_rows = first_row + jnp.arange(span, dtype=jnp.int32)
    offsets = jnp.arange(BAND, dtype=jnp.int32)
    inside = ((global_rows >= 0) & (global_rows < total))[:, None] & (
        global_rows[:, None] + offsets[None, :] < total
    )
    head_float = head.astype(jnp.float32)
    padded_width = BAND + 2 * DMAX

    def view_step(view, running):
        left = left_rows[view]
        right_cols = right_rows[view].T
        skewed = jnp.tile(right_cols, (1, span + 1))[:, : span * (width + 1)]
        skewed = skewed.reshape(PAIR_CH, span, width + 1)[:, :, :BAND]
        pairs = jax.nn.relu(left.T.astype(jnp.float32)[:, :, None] + skewed.astype(jnp.float32))
        pairs = jnp.where(inside[None], pairs, 0.0).astype(jnp.bfloat16)
        padded = jnp.pad(pairs, ((0, 0), (0, 0), (DMAX, DMAX)))
        summed = jnp.zeros((PAIR_CH, rows_out, BAND), jnp.float32)
        for row_tap in range(3):
            row_start = DMAX + (row_tap - 1) * dilate_pair
            row_piece = lax.dynamic_slice(
                padded, (jnp.int32(0), row_start, jnp.int32(0)), (PAIR_CH, rows_out, padded_width)
            )
            product = jnp.einsum(
                "cid,bce->beid", row_piece, pair_weight[row_tap], preferred_element_type=jnp.float32
            )
            for col_tap in range(3):
                col_start = DMAX + (col_tap - 1) * dilate_pair
                summed = summed + lax.dynamic_slice(
                    product[col_tap],
                    (jnp.int32(0), jnp.int32(0), col_start),
                    (PAIR_CH, rows_out, BAND),
                )
        hidden = jax.nn.relu(summed + pair_bias[:, None, None])
        return running + jnp.einsum("eid,e->id", hidden, head_float)

    running = lax.fori_loop(0, VIEWS, view_step, jnp.zeros((rows_out, BAND), jnp.float32))
    return running / VIEWS


def per_device(
    bins,
    conv_weight,
    conv_bias,
    pair_left,
    pair_right,
    pair_weight,
    pair_bias,
    head,
    shifts,
    flags,
    dilations,
):
    rows = bins.shape[0]
    segments = lax.axis_size("seg")
    position = lax.axis_index("seg")
    total = rows * segments
    kernels = view_kernels(conv_weight, flags)
    span = rows + 2 * DMAX
    rim = extended(bins, (("seg", 0),), HALO)
    left, right = trunk(
        rim, HALO, rows, shifts, dilations[0], kernels, conv_bias, pair_left, pair_right
    )
    carried = (
        jnp.concatenate([left, right], 2).transpose(1, 0, 2).reshape(rows, VIEWS * 2 * PAIR_CH)
    )
    behind = passed_along(carried, "seg", 1)
    front = carried
    reached = 1
    for step in range(AHEAD.bit_length() - 1):
        front = jnp.concatenate([front, passed_along(front, "seg", -reached)], 0)
        reached = reached * 2
    tail_rows = front[: (AHEAD - reached) * rows]
    front = jnp.concatenate([front, passed_along(tail_rows, "seg", -reached)], 0)
    window = jnp.concatenate([behind, front], 0)
    first = rows - DMAX
    grouped = window.reshape(-1, VIEWS, 2 * PAIR_CH).transpose(1, 0, 2)
    left_rows = grouped[:, first : first + span, :PAIR_CH]
    right_rows = grouped[:, first : first + span + BAND, PAIR_CH:]
    return pair_block(
        left_rows,
        right_rows,
        position * rows - DMAX,
        total,
        dilations[1],
        pair_weight,
        pair_bias,
        head,
    )


def solution(mesh):
    placed = (P(("groups", "seg"), None), P(), P(), P(), P(), P(), P(), P(), P(), P(), P())
    return jax.shard_map(
        per_device,
        mesh=mesh,
        in_specs=placed,
        out_specs=P(("groups", "seg"), None),
        check_vma=False,
    )
```

profile of v0, /device:TPU:0, one launch (start us, length us, event | category | flops | bytes accessed | tf_op | source)
XLA Modules:
  0.0 355.2 jit_solution(715674938283093827)
XLA Ops:
  11.8 5.1 %while.21 = (s32[]{:T(128)}, bf16[56,128]{1,0:T(8,128)(2,1)S(1)}, s32[4,2]{0,1:T(2,128)S(1)}, bf16[4,32,128]{2,1,0:T(8,128)(2,1)S(1)}, s32[]{:T(128)}) while((s32[]{:T(128)}, bf16[56,128]{1,0:T(8,128)(2,1)S(1)}, s32[4,2]{0,1:T(2,128)S(1)}, bf16[4,32,128]{2,1,0:T(8,128)(2,1)S(1)}, s32[]{:T(128)}) %tuple.95), condition=%wide.while_cond.1, body=%wide.while_body.1.sunk | while | flops 2 | bytes 16481 | solution.py:45
  16.9 5.1 %while.20 = (s32[]{:T(128)}, bf16[56,128]{1,0:T(8,128)(2,1)S(1)}, s32[4,2]{0,1:T(2,128)S(1)}, bf16[4,32,128]{2,1,0:T(8,128)(2,1)S(1)}, s32[]{:T(128)}) while((s32[]{:T(128)}, bf16[56,128]{1,0:T(8,128)(2,1)S(1)}, s32[4,2]{0,1:T(2,128)S(1)}, bf16[4,32,128]{2,1,0:T(8,128)(2,1)S(1)}, s32[]{:T(128)}) %tuple.107), condition=%wide.while_cond, body=%wide.while_body.sunk | while | flops 2 | bytes 16481 | solution.py:45
  22.0 5.1 %while.22 = (s32[]{:T(128)}, bf16[56,128]{1,0:T(8,128)(2,1)S(1)}, s32[4,2]{0,1:T(2,128)S(1)}, bf16[4,32,128]{2,1,0:T(8,128)(2,1)S(1)}, s32[]{:T(128)}) while((s32[]{:T(128)}, bf16[56,128]{1,0:T(8,128)(2,1)S(1)}, s32[4,2]{0,1:T(2,128)S(1)}, bf16[4,32,128]{2,1,0:T(8,128)(2,1)S(1)}, s32[]{:T(128)}) %tuple.108), condition=%wide.while_cond.2, body=%wide.while_body.2.sunk | while | flops 2 | bytes 16481 | solution.py:45
  30.7 4.5 %collective-permute-done.3 = bf16[32,384]{1,0:T(8,128)(2,1)S(1)} collective-permute-done((bf16[32,384]{1,0:T(8,128)(2,1)S(1)}, bf16[32,384]{1,0:T(8,128)(2,1)S(1)}, u32[]{:S(2)}, u32[]{:S(2)}) %collective-permute-start.3) | collective-permute-done | bytes 24608 | tf_op jit(solution)/shard_map/ppermute | solution.py:31
  36.5 5.1 %collective-permute-done.4 = bf16[64,384]{1,0:T(8,128)(2,1)S(1)} collective-permute-done((bf16[64,384]{1,0:T(8,128)(2,1)S(1)}, bf16[64,384]{1,0:T(8,128)(2,1)S(1)}, u32[]{:S(2)}, u32[]{:S(2)}) %collective-permute-start.4) | collective-permute-done | bytes 49184 | tf_op jit(solution)/shard_map/ppermute | solution.py:31
  43.0 6.9 %collective-permute-done.5 = bf16[128,384]{1,0:T(8,128)(2,1)S(1)} collective-permute-done((bf16[128,384]{1,0:T(8,128)(2,1)S(1)}, bf16[128,384]{1,0:T(8,128)(2,1)S(1)}, u32[]{:S(2)}, u32[]{:S(2)}) %collective-permute-start.5) | collective-permute-done | bytes 98336 | tf_op jit(solution)/shard_map/ppermute | solution.py:31
  58.7 4.8 %collective-permute-done.6 = bf16[256,384]{1,0:T(8,128)(2,1)S(1)} collective-permute-done((bf16[256,384]{1,0:T(8,128)(2,1)S(1)}, bf16[256,384]{1,0:T(8,128)(2,1)S(1)}, u32[]{:S(2)}, u32[]{:S(2)}) %collective-permute-start.6) | collective-permute-done | bytes 196640 | tf_op jit(solution)/shard_map/ppermute | solution.py:31
  65.3 288.5 %while.23 = (s32[]{:T(128)}, f32[32,512]{1,0:T(8,128)}, bf16[4,40,48]{2,1,0:T(8,128)(2,1)S(1)}, bf16[4,552,48]{1,2,0:T(8,128)(2,1)}, s32[]{:T(128)}, /*index=5*/...) while((s32[]{:T(128)}, f32[32,512]{1,0:T(8,128)}, ...), condition=%wide.region_1.2_spmd.clone, body=%wide.region_0.1_spmd.clone.sunk | while | flops 704542592 | bytes 148727280 | solution.py:103
  78.3 6.1 %convolution_bitcast_fusion.7 = f32[3,48,32,520]{3,1,2,0:T(8,128)} fusion(s32[]{:T(128)} %get-tuple-element.731, bf16[48,40,512]{2,0,1:T(8,128)(2,1)S(1)} %select_convert_fusion.2, bf16[3,3,48,48]{2,3,1,0:T(8,128)(2,1)S(1)} %copy-done.2), kind=kOutput, calls=%fused_computation.7.clone.1 | convolution fusion | flops 230031360 | bytes 11587588 | tf_op jit(solution)/shard_map/while/body/eval_jaxpr/cid,bce->beid/dot_general | solution.py:90
  84.3 6.1 %convolution_bitcast_fusion.6 = f32[3,48,32,520]{3,1,2,0:T(8,128)} fusion(bf16[48,40,512]{2,0,1:T(8,128)(2,1)S(1)} %select_convert_fusion.2, bf16[3,3,48,48]{2,3,1,0:T(8,128)(2,1)S(1)} %copy-done.2), kind=kOutput, calls=%fused_computation.8.clone.1 | convolution fusion | flops 230031360 | bytes 11587584 | tf_op jit(solution)/shard_map/while/body/eval_jaxpr/cid,bce->beid/dot_general | solution.py:90
  90.4 13.8 %fusion.89 = (f32[1,48,32,520]{3,1,2,0:T(8,128)S(1)}, f32[1,48,32,520]{3,1,2,0:T(8,128)S(1)}, f32[48,32,520]{2,0,1:T(8,128)}, f32[48,32,520]{2,0,1:T(8,128)}, f3...) fusion(f32[3,48,32,520]{3,1,2,0:T(8,128)} %convolution_bitcast_fusion.6, ...), kind=kLoop, calls=%fused_computation.97.clone.1 | loop fusion | bytes 38338560 | tf_op jit(solution)/shard_map/while/body/eval_jaxpr/slice | solution.py:96
  104.2 6.9 %convolution_bitcast_fusion.8 = f32[3,48,32,520]{3,1,0,2:T(8,128)} fusion(s32[]{:T(128)} %get-tuple-element.727, bf16[48,40,512]{2,0,1:T(8,128)(2,1)S(1)} %select_convert_fusion.2, bf16[3,3,48,48]{2,3,1,0:T(8,128)(2,1)} %get-tuple-element.728), kind=kOutput, calls=%fused_computation.9.clone.1 | convolution fusion | flops 230031360 | bytes 11588096 | tf_op jit(solution)/shard_map/while/body/eval_jaxpr/cid,bce->beid/dot_general | solution.py:90
  111.1 9.0 %fusion.90 = (f32[1,48,32,520]{3,1,0,2:T(8,128)}, f32[1,48,32,520]{3,1,0,2:T(8,128)}, f32[48,32,520]{2,0,1:T(8,128)}) fusion(f32[3,48,32,520]{3,1,0,2:T(8,128)} %convolution_bitcast_fusion.8), kind=kLoop, calls=%fused_computation.96.clone.1 | loop fusion | bytes 19169280 | tf_op jit(solution)/shard_map/while/body/eval_jaxpr/slice | solution.py:96
  120.1 16.7 %fusion.91 = f32[1,32,512]{2,0,1:T(1,128)S(1)} fusion(f32[48,32,520]{2,0,1:T(8,128)} %get-tuple-element.639, f32[48,32,520]{2,0,1:T(8,128)} %get-tuple-element.640, f32[48,32,520]{2,0,1:T(8,128)} %get-tuple-element.641, f32[1,48,32,520]{3,1,2,0:T(8,128)} %get-tuple-element.642, s32[]{:T(128)} %get-tuple-element.730, ...), kind=kOutput, calls=%fused_computation.18.clone.1 | convolution fusion | flops 9437184 | bytes 28379136 | tf_op jit(solution)/shard_map/while/body/eval_jaxpr/eid,e->id/dot_general | solution.py:101
  150.4 6.1 %convolution_bitcast_fusion.7 = f32[3,48,32,520]{3,1,2,0:T(8,128)} fusion(s32[]{:T(128)} %get-tuple-element.731, bf16[48,40,512]{2,0,1:T(8,128)(2,1)S(1)} %select_convert_fusion.2, bf16[3,3,48,48]{2,3,1,0:T(8,128)(2,1)S(1)} %copy-done.2), kind=kOutput, calls=%fused_computation.7.clone.1 | convolution fusion | flops 230031360 | bytes 11587588 | tf_op jit(solution)/shard_map/while/body/eval_jaxpr/cid,bce->beid/dot_general | solution.py:90
  156.4 6.1 %convolution_bitcast_fusion.6 = f32[3,48,32,520]{3,1,2,0:T(8,128)} fusion(bf16[48,40,512]{2,0,1:T(8,128)(2,1)S(1)} %select_convert_fusion.2, bf16[3,3,48,48]{2,3,1,0:T(8,128)(2,1)S(1)} %copy-done.2), kind=kOutput, calls=%fused_computation.8.clone.1 | convolution fusion | flops 230031360 | bytes 11587584 | tf_op jit(solution)/shard_map/while/body/eval_jaxpr/cid,bce->beid/dot_general | solution.py:90
  162.5 13.8 %fusion.89 = (f32[1,48,32,520]{3,1,2,0:T(8,128)S(1)}, f32[1,48,32,520]{3,1,2,0:T(8,128)S(1)}, f32[48,32,520]{2,0,1:T(8,128)}, f32[48,32,520]{2,0,1:T(8,128)}, f3...) fusion(f32[3,48,32,520]{3,1,2,0:T(8,128)} %convolution_bitcast_fusion.6, ...), kind=kLoop, calls=%fused_computation.97.clone.1 | loop fusion | bytes 38338560 | tf_op jit(solution)/shard_map/while/body/eval_jaxpr/slice | solution.py:96
  176.3 6.9 %convolution_bitcast_fusion.8 = f32[3,48,32,520]{3,1,0,2:T(8,128)} fusion(s32[]{:T(128)} %get-tuple-element.727, bf16[48,40,512]{2,0,1:T(8,128)(2,1)S(1)} %select_convert_fusion.2, bf16[3,3,48,48]{2,3,1,0:T(8,128)(2,1)} %get-tuple-element.728), kind=kOutput, calls=%fused_computation.9.clone.1 | convolution fusion | flops 230031360 | bytes 11588096 | tf_op jit(solution)/shard_map/while/body/eval_jaxpr/cid,bce->beid/dot_general | solution.py:90
  183.2 9.0 %fusion.90 = (f32[1,48,32,520]{3,1,0,2:T(8,128)}, f32[1,48,32,520]{3,1,0,2:T(8,128)}, f32[48,32,520]{2,0,1:T(8,128)}) fusion(f32[3,48,32,520]{3,1,0,2:T(8,128)} %convolution_bitcast_fusion.8), kind=kLoop, calls=%fused_computation.96.clone.1 | loop fusion | bytes 19169280 | tf_op jit(solution)/shard_map/while/body/eval_jaxpr/slice | solution.py:96
  192.2 16.7 %fusion.91 = f32[1,32,512]{2,0,1:T(1,128)S(1)} fusion(f32[48,32,520]{2,0,1:T(8,128)} %get-tuple-element.639, f32[48,32,520]{2,0,1:T(8,128)} %get-tuple-element.640, f32[48,32,520]{2,0,1:T(8,128)} %get-tuple-element.641, f32[1,48,32,520]{3,1,2,0:T(8,128)} %get-tuple-element.642, s32[]{:T(128)} %get-tuple-element.730, ...), kind=kOutput, calls=%fused_computation.18.clone.1 | convolution fusion | flops 9437184 | bytes 28379136 | tf_op jit(solution)/shard_map/while/body/eval_jaxpr/eid,e->id/dot_general | solution.py:101
  222.5 6.1 %convolution_bitcast_fusion.7 = f32[3,48,32,520]{3,1,2,0:T(8,128)} fusion(s32[]{:T(128)} %get-tuple-element.731, bf16[48,40,512]{2,0,1:T(8,128)(2,1)S(1)} %select_convert_fusion.2, bf16[3,3,48,48]{2,3,1,0:T(8,128)(2,1)S(1)} %copy-done.2), kind=kOutput, calls=%fused_computation.7.clone.1 | convolution fusion | flops 230031360 | bytes 11587588 | tf_op jit(solution)/shard_map/while/body/eval_jaxpr/cid,bce->beid/dot_general | solution.py:90
  228.6 6.1 %convolution_bitcast_fusion.6 = f32[3,48,32,520]{3,1,2,0:T(8,128)} fusion(bf16[48,40,512]{2,0,1:T(8,128)(2,1)S(1)} %select_convert_fusion.2, bf16[3,3,48,48]{2,3,1,0:T(8,128)(2,1)S(1)} %copy-done.2), kind=kOutput, calls=%fused_computation.8.clone.1 | convolution fusion | flops 230031360 | bytes 11587584 | tf_op jit(solution)/shard_map/while/body/eval_jaxpr/cid,bce->beid/dot_general | solution.py:90
  234.6 13.8 %fusion.89 = (f32[1,48,32,520]{3,1,2,0:T(8,128)S(1)}, f32[1,48,32,520]{3,1,2,0:T(8,128)S(1)}, f32[48,32,520]{2,0,1:T(8,128)}, f32[48,32,520]{2,0,1:T(8,128)}, f3...) fusion(f32[3,48,32,520]{3,1,2,0:T(8,128)} %convolution_bitcast_fusion.6, ...), kind=kLoop, calls=%fused_computation.97.clone.1 | loop fusion | bytes 38338560 | tf_op jit(solution)/shard_map/while/body/eval_jaxpr/slice | solution.py:96
  248.4 6.9 %convolution_bitcast_fusion.8 = f32[3,48,32,520]{3,1,0,2:T(8,128)} fusion(s32[]{:T(128)} %get-tuple-element.727, bf16[48,40,512]{2,0,1:T(8,128)(2,1)S(1)} %select_convert_fusion.2, bf16[3,3,48,48]{2,3,1,0:T(8,128)(2,1)} %get-tuple-element.728), kind=kOutput, calls=%fused_computation.9.clone.1 | convolution fusion | flops 230031360 | bytes 11588096 | tf_op jit(solution)/shard_map/while/body/eval_jaxpr/cid,bce->beid/dot_general | solution.py:90
  255.3 9.0 %fusion.90 = (f32[1,48,32,520]{3,1,0,2:T(8,128)}, f32[1,48,32,520]{3,1,0,2:T(8,128)}, f32[48,32,520]{2,0,1:T(8,128)}) fusion(f32[3,48,32,520]{3,1,0,2:T(8,128)} %convolution_bitcast_fusion.8), kind=kLoop, calls=%fused_computation.96.clone.1 | loop fusion | bytes 19169280 | tf_op jit(solution)/shard_map/while/body/eval_jaxpr/slice | solution.py:96
  264.3 16.7 %fusion.91 = f32[1,32,512]{2,0,1:T(1,128)S(1)} fusion(f32[48,32,520]{2,0,1:T(8,128)} %get-tuple-element.639, f32[48,32,520]{2,0,1:T(8,128)} %get-tuple-element.640, f32[48,32,520]{2,0,1:T(8,128)} %get-tuple-element.641, f32[1,48,32,520]{3,1,2,0:T(8,128)} %get-tuple-element.642, s32[]{:T(128)} %get-tuple-element.730, ...), kind=kOutput, calls=%fused_computation.18.clone.1 | convolution fusion | flops 9437184 | bytes 28379136 | tf_op jit(solution)/shard_map/while/body/eval_jaxpr/eid,e->id/dot_general | solution.py:101
  294.6 6.1 %convolution_bitcast_fusion.7 = f32[3,48,32,520]{3,1,2,0:T(8,128)} fusion(s32[]{:T(128)} %get-tuple-element.731, bf16[48,40,512]{2,0,1:T(8,128)(2,1)S(1)} %select_convert_fusion.2, bf16[3,3,48,48]{2,3,1,0:T(8,128)(2,1)S(1)} %copy-done.2), kind=kOutput, calls=%fused_computation.7.clone.1 | convolution fusion | flops 230031360 | bytes 11587588 | tf_op jit(solution)/shard_map/while/body/eval_jaxpr/cid,bce->beid/dot_general | solution.py:90
  300.7 6.1 %convolution_bitcast_fusion.6 = f32[3,48,32,520]{3,1,2,0:T(8,128)} fusion(bf16[48,40,512]{2,0,1:T(8,128)(2,1)S(1)} %select_convert_fusion.2, bf16[3,3,48,48]{2,3,1,0:T(8,128)(2,1)S(1)} %copy-done.2), kind=kOutput, calls=%fused_computation.8.clone.1 | convolution fusion | flops 230031360 | bytes 11587584 | tf_op jit(solution)/shard_map/while/body/eval_jaxpr/cid,bce->beid/dot_general | solution.py:90
  306.7 13.8 %fusion.89 = (f32[1,48,32,520]{3,1,2,0:T(8,128)S(1)}, f32[1,48,32,520]{3,1,2,0:T(8,128)S(1)}, f32[48,32,520]{2,0,1:T(8,128)}, f32[48,32,520]{2,0,1:T(8,128)}, f3...) fusion(f32[3,48,32,520]{3,1,2,0:T(8,128)} %convolution_bitcast_fusion.6, ...), kind=kLoop, calls=%fused_computation.97.clone.1 | loop fusion | bytes 38338560 | tf_op jit(solution)/shard_map/while/body/eval_jaxpr/slice | solution.py:96
  320.5 6.9 %convolution_bitcast_fusion.8 = f32[3,48,32,520]{3,1,0,2:T(8,128)} fusion(s32[]{:T(128)} %get-tuple-element.727, bf16[48,40,512]{2,0,1:T(8,128)(2,1)S(1)} %select_convert_fusion.2, bf16[3,3,48,48]{2,3,1,0:T(8,128)(2,1)} %get-tuple-element.728), kind=kOutput, calls=%fused_computation.9.clone.1 | convolution fusion | flops 230031360 | bytes 11588096 | tf_op jit(solution)/shard_map/while/body/eval_jaxpr/cid,bce->beid/dot_general | solution.py:90
  327.4 9.0 %fusion.90 = (f32[1,48,32,520]{3,1,0,2:T(8,128)}, f32[1,48,32,520]{3,1,0,2:T(8,128)}, f32[48,32,520]{2,0,1:T(8,128)}) fusion(f32[3,48,32,520]{3,1,0,2:T(8,128)} %convolution_bitcast_fusion.8), kind=kLoop, calls=%fused_computation.96.clone.1 | loop fusion | bytes 19169280 | tf_op jit(solution)/shard_map/while/body/eval_jaxpr/slice | solution.py:96
  336.4 16.7 %fusion.91 = f32[1,32,512]{2,0,1:T(1,128)S(1)} fusion(f32[48,32,520]{2,0,1:T(8,128)} %get-tuple-element.639, f32[48,32,520]{2,0,1:T(8,128)} %get-tuple-element.640, f32[48,32,520]{2,0,1:T(8,128)} %get-tuple-element.641, f32[1,48,32,520]{3,1,2,0:T(8,128)} %get-tuple-element.642, s32[]{:T(128)} %get-tuple-element.730, ...), kind=kOutput, calls=%fused_computation.18.clone.1 | convolution fusion | flops 9437184 | bytes 28379136 | tf_op jit(solution)/shard_map/while/body/eval_jaxpr/eid,e->id/dot_general | solution.py:101
  (169 shorter events, 95.9 us)
Async XLA Ops:
  0.0 28.2 %copy-start = (bf16[128,48]{0,1:T(8,128)(2,1)S(1)}, bf16[128,48]{0,1:T(8,128)(2,1)}, u32[]{:S(2)}) copy-start(bf16[128,48]{0,1:T(8,128)(2,1)} %param.17) | copy-start | bytes 36868
  0.0 65.2 %copy-start.5 = (f32[48]{0:T(128)S(1)}, f32[48]{0:T(128)}, u32[]{:S(2)}) copy-start(f32[48]{0:T(128)} %param.19) | copy-start | bytes 580
  0.0 65.3 %copy-start.6 = (bf16[48]{0:T(256)(128)(2,1)S(1)}, bf16[48]{0:T(256)(128)(2,1)}, u32[]{:S(2)}) copy-start(bf16[48]{0:T(256)(128)(2,1)} %param.20) | copy-start | bytes 292
  0.8 10.3 %collective-permute-start = (bf16[12,128]{1,0:T(8,128)(2,1)S(1)}, bf16[12,128]{1,0:T(8,128)(2,1)S(1)}, u32[]{:S(2)}, u32[]{:S(2)}) collective-permute-start(bf16[12,128]{1,0:T(8,128)(2,1)S(1)} %get-tuple-element.469), channel_id=1, source_target_pairs={{0,1},{1,2},{2,3},{3,4},{4,5},{5,6},{6,7},{7,8},{8,9},{9,10},{10,1... | collective-permute-start | bytes 9224 | tf_op jit(solution)/shard_map/ppermute | solution.py:22
  3.1 7.9 %collective-permute-start.1 = (bf16[12,128]{1,0:T(8,128)(2,1)S(1)}, bf16[12,128]{1,0:T(8,128)(2,1)S(1)}, u32[]{:S(2)}, u32[]{:S(2)}) collective-permute-start(bf16[12,128]{1,0:T(8,128)(2,1)S(1)} %get-tuple-element.470), channel_id=1, source_target_pairs={{1,0},{2,1},{3,2},{4,3},{5,4},{6,5},{7,6},{8,7},{9,8},{10,9},{11,1... | collective-permute-start | bytes 9224 | tf_op jit(solution)/shard_map/ppermute | solution.py:23
  29.4 5.9 %collective-permute-start.3 = (bf16[32,384]{1,0:T(8,128)(2,1)S(1)}, bf16[32,384]{1,0:T(8,128)(2,1)S(1)}, u32[]{:S(2)}, u32[]{:S(2)}) collective-permute-start(bf16[32,384]{1,0:T(8,128)(2,1)S(1)} %reshape.101), channel_id=1, source_target_pairs={{1,0},{2,1},{3,2},{4,3},{5,4},{6,5},{7,6},{8,7},{9,8},{10,9},{11,1... | collective-permute-start | bytes 73736 | tf_op jit(solution)/shard_map/ppermute | solution.py:31
  35.2 6.4 %collective-permute-start.4 = (bf16[64,384]{1,0:T(8,128)(2,1)S(1)}, bf16[64,384]{1,0:T(8,128)(2,1)S(1)}, u32[]{:S(2)}, u32[]{:S(2)}) collective-permute-start(bf16[64,384]{1,0:T(8,128)(2,1)S(1)} %constant_dynamic-update-slice_fusion), channel_id=1, source_target_pairs={{2,0},{3,1},{4,2},{5,3},{6,4},{7,5},{8,6},{9,7},{10,8},{11,9},{12,... | collective-permute-start | bytes 147464 | tf_op jit(solution)/shard_map/ppermute | solution.py:31
  41.7 8.2 %collective-permute-start.5 = (bf16[128,384]{1,0:T(8,128)(2,1)S(1)}, bf16[128,384]{1,0:T(8,128)(2,1)S(1)}, u32[]{:S(2)}, u32[]{:S(2)}) collective-permute-start(bf16[128,384]{1,0:T(8,128)(2,1)S(1)} %pad_maximum_fusion.1), channel_id=1, source_target_pairs={{4,0},{5,1},{6,2},{7,3},{8,4},{9,5},{10,6},{11,7},{12,8},{13,9},{1... | collective-permute-start | bytes 294920 | tf_op jit(solution)/shard_map/ppermute | solution.py:31
  49.9 13.6 %collective-permute-start.6 = (bf16[256,384]{1,0:T(8,128)(2,1)S(1)}, bf16[256,384]{1,0:T(8,128)(2,1)S(1)}, u32[]{:S(2)}, u32[]{:S(2)}) collective-permute-start(bf16[256,384]{1,0:T(8,128)(2,1)S(1)} %pad_maximum_fusion), channel_id=1, source_target_pairs={{8,0},{9,1},{10,2},{11,3},{12,4},{13,5},{14,6},{15,7},{24,16},{25,... | collective-permute-start | bytes 589832 | tf_op jit(solution)/shard_map/ppermute | solution.py:31
  51.3 7.0 %collective-permute-start.2 = (bf16[32,384]{1,0:T(8,128)(2,1)S(1)}, bf16[32,384]{1,0:T(8,128)(2,1)S(1)}, u32[]{:S(2)}, u32[]{:S(2)}) collective-permute-start(bf16[32,384]{1,0:T(8,128)(2,1)S(1)} %reshape.101), channel_id=1, source_target_pairs={{0,1},{1,2},{2,3},{3,4},{4,5},{5,6},{6,7},{7,8},{8,9},{9,10},{10,1... | collective-permute-start | bytes 73736 | tf_op jit(solution)/shard_map/ppermute | solution.py:31
  52.9 5.6 %collective-permute-start.7 = (bf16[64,384]{1,0:T(8,128)(2,1)S(1)}, bf16[64,384]{1,0:T(8,128)(2,1)S(1)}, u32[]{:S(2)}, u32[]{:S(2)}) collective-permute-start(bf16[64,384]{1,0:T(8,128)(2,1)S(1)} %constant_dynamic-update-slice_fusion), channel_id=1, source_target_pairs={} | collective-permute-start | bytes 147464 | tf_op jit(solution)/shard_map/ppermute | solution.py:31
  69.8 1.6 slice-start
  75.6 1.5 slice-start.1
  75.6 2.7 copy-start.2
  120.1 16.7 %copy-start.3 = (f32[32,512]{1,0:T(8,128)S(1)}, f32[32,512]{1,0:T(8,128)}, u32[]{:S(2)}) copy-start(f32[32,512]{1,0:T(8,128)} %get-tuple-element.709) | copy-start | bytes 196612 | tf_op jit(solution)/shard_map/while
  136.8 0.6 copy-start.4
  141.9 1.6 slice-start
  147.7 1.5 slice-start.1
  147.7 2.7 copy-start.2
  192.2 16.7 %copy-start.3 = (f32[32,512]{1,0:T(8,128)S(1)}, f32[32,512]{1,0:T(8,128)}, u32[]{:S(2)}) copy-start(f32[32,512]{1,0:T(8,128)} %get-tuple-element.709) | copy-start | bytes 196612 | tf_op jit(solution)/shard_map/while
  208.9 0.6 copy-start.4
  214.0 1.6 slice-start
  219.8 1.5 slice-start.1
  219.8 2.7 copy-start.2
  264.3 16.7 %copy-start.3 = (f32[32,512]{1,0:T(8,128)S(1)}, f32[32,512]{1,0:T(8,128)}, u32[]{:S(2)}) copy-start(f32[32,512]{1,0:T(8,128)} %get-tuple-element.709) | copy-start | bytes 196612 | tf_op jit(solution)/shard_map/while
  281.0 0.6 copy-start.4
  286.1 1.6 slice-start
  291.9 1.5 slice-start.1
  291.9 2.7 copy-start.2
  336.4 16.7 %copy-start.3 = (f32[32,512]{1,0:T(8,128)S(1)}, f32[32,512]{1,0:T(8,128)}, u32[]{:S(2)}) copy-start(f32[32,512]{1,0:T(8,128)} %get-tuple-element.709) | copy-start | bytes 196612 | tf_op jit(solution)/shard_map/while
  353.1 0.6 copy-start.4
  353.7 1.5 copy-start.1
where the time goes:
time: 357 us; the launch traced here: 355 us
  local copies, waits for them, and re-layouts  164 us (46%)
  matrix products  145 us (41%)
  waiting for transfers between devices  21.4 us (6%)
  starting transfers between devices  11.1 us (3%)
  other arithmetic  10.3 us (3%)
  between operations  3.65 us (1%)
    slice x8, local copies, waits for them, and re-layouts, view_step(): product[col_tap]  91.1 us
    dot_general x12, matrix products, view_step(): jnp.einsum('cid,bce->beid', row_piece, pair_weight[row_tap], preferred_el...  76 us
    dot_general x4, matrix products, view_step(): return running + jnp.einsum('eid,e->id', hidden, head_float)  66.8 us
    ppermute x6, waiting for transfers between devices, passed_along(): return lax.ppermute(block, axis, route)  21.4 us
    reshape x4, local copies, waits for them, and re-layouts, view_step(): skewed = skewed.reshape(PAIR_CH, span, width + 1)[:, :, :BAND]  16.7 us
    gather x36, local copies, waits for them, and re-layouts  15.1 us
    another operation x8, local copies, waits for them, and re-layouts, view_step(): skewed = jnp.tile(right_cols, (1, span + 1))[:, :span * (width + 1)]  14.7 us
    ppermute x6, starting transfers between devices, passed_along(): return lax.ppermute(block, axis, route)  7.47 us
  transfers between devices with their start and end apart: 8, of which 4 were waited for; matrix products, arithmetic and copies ran while one was open for 2% of the time, Pallas kernels for 0%

commit v1 on v0

v1 whole, which is shorter than its diff:
```python
import functools

import jax
import jax.numpy as jnp
from jax import lax
from jax.experimental import pallas as pl
from jax.experimental.pallas import tpu as pltpu
from jax.sharding import PartitionSpec as P

CHANNELS = 128
PAIR_CH = 48
BAND = 512
VIEWS = 4
DMAX = 4
HALO = 12
EDGE = DMAX + HALO
LANES = 128
OUT = -1e30


def taken(tiles, amount):
    lane = lax.broadcasted_iota(jnp.int32, tiles[0].shape, 1)
    turned = [pltpu.roll(tile, (LANES - amount) % LANES, 1) for tile in tiles]
    keep = lane < LANES - amount
    return [
        jnp.where(keep, turned[t], turned[min(t + 1, len(tiles) - 1)]) for t in range(len(tiles))
    ]


def kernel(
    rows,
    total,
    scalars,
    bins,
    conv,
    conv_bias,
    project,
    pair,
    pair_bias,
    head,
    out,
    padded,
    sides,
    pairs,
    found,
):
    reach = rows + 2 * DMAX + 2
    span = -(-(BAND + rows + 2 * EDGE) // 16) * 16
    first = scalars[0]
    seq_rate = scalars[1]
    pair_rate = scalars[2]

    padded[0:EDGE, :] = jnp.zeros((EDGE, CHANNELS), jnp.float32)
    padded[EDGE : EDGE + total, :] = bins[...].astype(jnp.float32)
    padded[EDGE + total :, :] = jnp.zeros(
        (padded.shape[0] - EDGE - total, CHANNELS), jnp.float32
    )
    taps = [
        padded[pl.ds(first + DMAX + (tap - 1) * seq_rate, span), :] for tap in range(3)
    ]
    stacked = jnp.concatenate([tap.astype(jnp.bfloat16) for tap in taps], 1)
    mixed = jnp.dot(stacked, conv[...], preferred_element_type=jnp.float32)
    for flag in range(2):
        part = mixed[:, flag * CHANNELS : (flag + 1) * CHANNELS]
        feature = (taps[1] + jnp.maximum(part + conv_bias[...], 0.0)).astype(jnp.bfloat16)
        both = lax.dot_general(
            project[...], feature, (((1,), (1,)), ((), ())), preferred_element_type=jnp.float32
        )
        sides[flag, :, 0:span] = both.astype(jnp.bfloat16).astype(jnp.float32)

    width = sides.shape[2]

    def prepare(view, carry):
        shift = scalars[3 + view]
        flag = scalars[3 + VIEWS + view]
        both = sides[flag]
        moved = taken(
            [both[:, t * LANES : (t + 1) * LANES] for t in range(width // LANES)],
            shift + HALO - DMAX,
        )
        lane = lax.broadcasted_iota(jnp.int32, (PAIR_CH, LANES), 1)
        place = first - DMAX + lane
        left = jnp.where((place >= 0) & (place < total), moved[0][:PAIR_CH], OUT)
        right = jnp.concatenate(
            [
                jnp.where(place + t * LANES < total, moved[t][PAIR_CH:], OUT)
                for t in range(width // LANES)
            ],
            1,
        )
        for row in range(reach):
            value = left[:, row : row + 1] + right[:, row : row + BAND]
            pairs[view, row] = jnp.maximum(value, 0.0).astype(jnp.bfloat16)
        return carry

    lax.fori_loop(0, VIEWS, prepare, 0)

    lane = lax.broadcasted_iota(jnp.int32, (PAIR_CH, LANES), 1)
    tiles = BAND // LANES

    def group(number, carry):
        block = lax.div(number, pair_rate)
        base = number + block * pair_rate
        sums = [[None] * tiles for _ in range(2)]
        for view in range(VIEWS):
            stack = jnp.concatenate(
                [pairs[view, base + DMAX + (cell - 1) * pair_rate] for cell in range(4)], 0
            )
            product = jnp.dot(pair[...], stack, preferred_element_type=jnp.float32)
            for half in range(2):
                low, mid, high = [
                    product[(3 * half + tap) * PAIR_CH : (3 * half + tap + 1) * PAIR_CH]
                    for tap in range(3)
                ]
                up = [
                    pltpu.roll(low[:, t * LANES : (t + 1) * LANES], pair_rate, 1)
                    for t in range(tiles)
                ]
                down = [
                    pltpu.roll(high[:, t * LANES : (t + 1) * LANES], LANES - pair_rate, 1)
                    for t in range(tiles)
                ]
                for t in range(tiles):
                    before = up[t - 1] if t else 0.0
                    after = down[t + 1] if t + 1 < tiles else 0.0
                    value = (
                        mid[:, t * LANES : (t + 1) * LANES]
                        + jnp.where(lane < pair_rate, before, up[t])
                        + jnp.where(lane >= LANES - pair_rate, after, down[t])
                    )
                    hidden = jnp.maximum(value + pair_bias[...], 0.0)
                    sums[half][t] = hidden if view == 0 else sums[half][t] + hidden
        for half in range(2):
            row = jnp.concatenate(
                [
                    jnp.sum(sums[half][t] * head[...], axis=0, keepdims=True)
                    for t in range(tiles)
                ],
                1,
            )
            found[pl.ds(base + half * pair_rate, 1), :] = row * (1.0 / VIEWS)
        return carry

    blocks = rows // (2 * pair_rate)
    left_over = rows - blocks * 2 * pair_rate
    groups = blocks * pair_rate + jnp.minimum(left_over, pair_rate)
    lax.fori_loop(0, groups, group, 0)
    out[...] = found[0:rows, :]


def per_device(
    bins,
    conv_weight,
    conv_bias,
    pair_left,
    pair_right,
    pair_weight,
    pair_bias,
    head,
    shifts,
    flags,
    dilations,
):
    rows = bins.shape[0]
    segments = lax.axis_size("seg")
    total = rows * segments
    first = lax.axis_index("seg") * rows
    every = lax.all_to_all(
        jnp.broadcast_to(bins[None], (segments,) + bins.shape), "seg", 0, 0
    ).reshape(total, CHANNELS)
    taps = conv_weight.reshape(3 * CHANNELS, CHANNELS)
    conv = jnp.concatenate([taps, taps[::-1]], 1)
    project = jnp.concatenate([pair_left, pair_right], 1).T
    by_out = pair_weight.transpose(1, 3, 0, 2).reshape(3 * PAIR_CH, 3 * PAIR_CH)
    pair = jnp.concatenate(
        [
            jnp.pad(by_out, ((0, 0), (0, PAIR_CH))),
            jnp.pad(by_out, ((0, 0), (PAIR_CH, 0))),
        ],
        0,
    )
    scalars = jnp.concatenate([first[None], dilations, shifts, flags]).astype(jnp.int32)
    span = -(-(BAND + rows + 2 * EDGE) // 16) * 16
    width = -(-span // LANES) * LANES
    whole = pl.BlockSpec(memory_space=pltpu.VMEM)
    return pl.pallas_call(
        functools.partial(kernel, rows, total),
        out_shape=jax.ShapeDtypeStruct((rows, BAND), jnp.float32),
        in_specs=[pl.BlockSpec(memory_space=pltpu.SMEM)] + [whole] * 7,
        out_specs=whole,
        scratch_shapes=[
            pltpu.VMEM((total + span + EDGE, CHANNELS), jnp.float32),
            pltpu.VMEM((2, 2 * PAIR_CH, width), jnp.float32),
            pltpu.VMEM((VIEWS, rows + 2 * DMAX + 2, PAIR_CH, BAND), jnp.bfloat16),
            pltpu.VMEM((rows + DMAX + 4, BAND), jnp.float32),
        ],
        compiler_params=pltpu.CompilerParams(vmem_limit_bytes=40 << 20),
    )(
        scalars,
        every,
        conv,
        conv_bias[None],
        project,
        pair,
        jnp.broadcast_to(pair_bias[:, None], (PAIR_CH, LANES)),
        jnp.broadcast_to(head.astype(jnp.float32)[:, None], (PAIR_CH, LANES)),
    )


def solution(mesh):
    placed = (P(("groups", "seg"), None), P(), P(), P(), P(), P(), P(), P(), P(), P(), P())
    return jax.shard_map(
        per_device,
        mesh=mesh,
        in_specs=placed,
        out_specs=P(("groups", "seg"), None),
        check_vma=False,
    )
```

time: 357 us -> 45.4 us (0.13)
  local copies, waits for them, and re-layouts: 164 us -> 3.83 us
  matrix products: 145 us -> 0 us
  Pallas kernels: 0 us -> 26.8 us
  waiting for transfers between devices: 21.4 us -> 6.54 us
  other arithmetic: 10.3 us -> 0.2 us
  starting transfers between devices: 11.1 us -> 7.52 us
    dot_general x21 -> x0, matrix products: 145 us -> none  [the longest x12 76 us: view_step(): jnp.einsum('cid,bce->beid', row_piece, pair_weight[row_tap], preferred_el...]
    slice x28 -> x0, local copies, waits for them, and re-layouts: 106 us -> none  [the longest x8 91.1 us: view_step(): product[col_tap]]
    pallas_call x0 -> x1, Pallas kernels: none -> 26.8 us  [per_device(): pl.pallas_call(functools.partial(kernel, rows, total), out_shape=jax.Shap...]
    ppermute x8 -> x0, waiting for transfers between devices: 21.4 us -> none  [the longest x6 21.4 us: passed_along(): return lax.ppermute(block, axis, route)]
    reshape x5 -> x1, local copies, waits for them, and re-layouts: 16.8 us -> 0.12 us  [per_device(): by_out = pair_weight.transpose(1, 3, 0, 2).reshape(3 * PAIR_CH, 3 * PAIR_CH)]
    gather x36 -> x0, local copies, waits for them, and re-layouts: 15.1 us -> none
    another operation x8 -> x0, local copies, waits for them, and re-layouts: 14.7 us -> none  [view_step(): skewed = jnp.tile(right_cols, (1, span + 1))[:, :span * (width + 1)]]
    ppermute x8 -> x0, starting transfers between devices: 11.1 us -> none  [the longest x6 7.47 us: passed_along(): return lax.ppermute(block, axis, route)]
  transfers between devices with their start and end apart: 8 -> 1, of which waited for: 4 -> 1; matrix products, arithmetic and copies ran while one was open for 2% -> 1% of each run, Pallas kernels for 0% -> 0%
where the time goes in v1:
time: 45.4 us; the launch traced here: 45 us
  Pallas kernels  26.8 us (59%)
  starting transfers between devices  7.52 us (17%)
  waiting for transfers between devices  6.54 us (14%)
  local copies, waits for them, and re-layouts  3.83 us (8%)
    pallas_call x1, Pallas kernels, per_device(): pl.pallas_call(functools.partial(kernel, rows, total), out_shape=jax.Shap...  26.8 us
    all_to_all x1, starting transfers between devices, per_device(): lax.all_to_all(jnp.broadcast_to(bins[None], (segments,) + bins.shape), 's...  7.52 us
    all_to_all x1, waiting for transfers between devices, per_device(): lax.all_to_all(jnp.broadcast_to(bins[None], (segments,) + bins.shape), 's...  6.54 us
    unnamed x20, local copies, waits for them, and re-layouts  1.97 us
    broadcast_in_dim x1, local copies, waits for them, and re-layouts, per_device(): jnp.broadcast_to(bins[None], (segments,) + bins.shape)  1.35 us
  transfers between devices with their start and end apart: 1, of which 1 were waited for; matrix products, arithmetic and copies ran while one was open for 1% of the time, Pallas kernels for 0%

profile of v1, /device:TPU:0, one launch (start us, length us, event | category | flops | bytes accessed | tf_op | source)
XLA Modules:
  0.0 45.0 jit_solution(16482128925715909209)
XLA Ops:
  0.0 1.3 %broadcast_in_dim.11 = bf16[16,32,128]{2,1,0:T(8,128)(2,1)} broadcast(bf16[32,128]{1,0:T(8,128)(2,1)} %param.11), dimensions={1,2} | broadcast | bytes 139264 | tf_op jit(solution)/shard_map/broadcast_in_dim | solution.py:169
  1.4 0.0 copy-start.3
  1.4 0.0 copy-start.4
  1.4 0.0 copy-start.1
  1.4 7.5 %all-to-all-start = ((bf16[16,32,128]{2,1,0:T(8,128)(2,1)}), bf16[16,32,128]{2,1,0:T(8,128)(2,1)S(1)}, u32[]{:S(2)}, u32[]{:S(2)}) async-start(bf16[16,32,128]{2,1,0:T(8,128)(2,1)} %broadcast_in_dim.11), calls=%async_computation | async-start | bytes 262144 | tf_op jit(solution)/shard_map/all_to_all | solution.py:168
  8.9 0.0 copy-done.3
  8.9 0.0 copy-done.4
  8.9 0.0 copy-start.5
  8.9 0.0 copy-start.6
  8.9 0.0 copy-start.7
  9.0 0.0 copy-start.2
  9.0 0.6 %copy-done.5 = s32[4]{0:T(128)S(1)} copy-done((s32[4]{0:T(128)S(1)}, s32[4]{0:T(128)}, u32[]{:S(2)}) %copy-start.5) | copy-done | bytes 40
  9.6 0.0 copy-done.6
  9.6 0.0 copy-done.7
  9.6 0.1 pad_add_fusion.scalars
  9.7 0.0 copy-done.1
  9.7 0.1 rev.3
  9.8 0.1 copy-done.2
  9.9 0.1 copy.13
  10.0 0.1 reshape.14
  10.1 0.1 fusion.2.pair
  10.3 0.0 copy-start.8
  10.3 6.5 %all-to-all-done = bf16[16,32,128]{2,1,0:T(8,128)(2,1)S(1)} async-done(((bf16[16,32,128]{2,1,0:T(8,128)(2,1)}), bf16[16,32,128]{2,1,0:T(8,128)(2,1)S(1)}, u32[]{:S(2)}, u32[]{:S(2)}) %all-to-all-start) | async-done | bytes 131104 | tf_op jit(solution)/shard_map/all_to_all | solution.py:168
  16.8 0.0 copy-done.8
  16.8 0.0 copy-start.9
  16.8 0.1 broadcast_in_dim.13.pair_bias
  16.9 0.6 %copy-done.9 = bf16[48]{0:T(256)(128)(2,1)S(1)} copy-done((bf16[48]{0:T(256)(128)(2,1)S(1)}, bf16[48]{0:T(256)(128)(2,1)}, u32[]{:S(2)}) %copy-start.9) | copy-done | bytes 120
  17.5 0.1 broadcast_in_dim.28.head
  17.5 0.0 copy-start
  17.6 0.7 %copy-done = f32[128]{0:T(128)S(1)} copy-done((f32[128]{0:T(128)S(1)}, f32[128]{0:T(128)}, u32[]{:S(2)}) %copy-start) | copy-done | bytes 536
  18.2 26.8 %shard_map.109 = f32[32,512]{1,0:T(8,128)} custom-call(s32[11]{0:T(128)S(1)} %pad_add_fusion.scalars, bf16[512,128]{1,0:T(8,128)(2,1)S(1)} %bitcast.7, bf16[384,256]{1,0:T(8,128)(2,1)S(1)} %pad_maximum_fusion.conv, f32[1,128]{1,0:T(1,128)S(1)} %bitcast.8, bf16[96,128]{1,0:T(8,128)(2,1)S(1)} %maximum_bitcast_fusion.project, bf16[288,192]{1,0:T(8,128)(2,1)S(1)} %fusion.2.pair, ...), custom_call_target="tpu_custom_call" | custom-call | tf_op jit(solution)/shard_map/pallas_call | solution.py:186
  (2 shorter events, 0.0 us)
Async XLA Ops:
  1.4 7.5 %copy-start.3 = (bf16[128,48]{0,1:T(8,128)(2,1)S(1)}, bf16[128,48]{0,1:T(8,128)(2,1)}, u32[]{:S(2)}) copy-start(bf16[128,48]{0,1:T(8,128)(2,1)} %param.15) | copy-start | bytes 36868
  1.4 7.5 %copy-start.4 = (bf16[128,48]{0,1:T(8,128)(2,1)S(1)}, bf16[128,48]{0,1:T(8,128)(2,1)}, u32[]{:S(2)}) copy-start(bf16[128,48]{0,1:T(8,128)(2,1)} %param.14) | copy-start | bytes 36868
  1.4 8.3 %copy-start.1 = (bf16[3,128,128]{2,1,0:T(8,128)(2,1)S(1)}, bf16[3,128,128]{2,1,0:T(8,128)(2,1)}, u32[]{:S(2)}) copy-start(bf16[3,128,128]{2,1,0:T(8,128)(2,1)} %param.12) | copy-start | bytes 294916
  1.4 15.5 %all-to-all-start = ((bf16[16,32,128]{2,1,0:T(8,128)(2,1)}), bf16[16,32,128]{2,1,0:T(8,128)(2,1)S(1)}, u32[]{:S(2)}, u32[]{:S(2)}) async-start(bf16[16,32,128]{2,1,0:T(8,128)(2,1)} %broadcast_in_dim.11), calls=%async_computation | async-start | bytes 262144 | tf_op jit(solution)/shard_map/all_to_all | solution.py:168
  8.9 0.7 %copy-start.5 = (s32[4]{0:T(128)S(1)}, s32[4]{0:T(128)}, u32[]{:S(2)}) copy-start(s32[4]{0:T(128)} %param.20) | copy-start | bytes 52
  8.9 0.7 %copy-start.6 = (s32[4]{0:T(128)S(1)}, s32[4]{0:T(128)}, u32[]{:S(2)}) copy-start(s32[4]{0:T(128)} %param.19) | copy-start | bytes 52
  8.9 0.7 %copy-start.7 = (s32[2]{0:T(128)S(1)}, s32[2]{0:T(128)}, u32[]{:S(2)}) copy-start(s32[2]{0:T(128)} %param.21) | copy-start | bytes 28
  9.0 0.9 %copy-start.2 = (bf16[3,3,48,48]{3,2,1,0:T(8,128)(2,1)S(1)}, bf16[3,3,48,48]{3,2,1,0:T(8,128)(2,1)}, u32[]{:S(2)}) copy-start(bf16[3,3,48,48]{3,2,1,0:T(8,128)(2,1)} %param.16) | copy-start | bytes 124420
  10.3 6.6 %copy-start.8 = (f32[48]{0:T(128)S(1)}, f32[48]{0:T(128)}, u32[]{:S(2)}) copy-start(f32[48]{0:T(128)} %param.17) | copy-start | bytes 580
  16.8 0.7 %copy-start.9 = (bf16[48]{0:T(256)(128)(2,1)S(1)}, bf16[48]{0:T(256)(128)(2,1)}, u32[]{:S(2)}) copy-start(bf16[48]{0:T(256)(128)(2,1)} %param.18) | copy-start | bytes 292
  17.5 0.7 %copy-start = (f32[128]{0:T(128)S(1)}, f32[128]{0:T(128)}, u32[]{:S(2)}) copy-start(f32[128]{0:T(128)} %param.13) | copy-start | bytes 1540

commit v2 on v1

v2 whole, which is shorter than its diff:
```python
import functools

import jax
import jax.numpy as jnp
from jax import lax
from jax.experimental import pallas as pl
from jax.experimental.pallas import tpu as pltpu
from jax.sharding import PartitionSpec as P

CHANNELS = 128
PAIR_CH = 48
BAND = 512
VIEWS = 4
DMAX = 4
HALO = 20
EDGE = DMAX + HALO
LANES = 128
OUT = -1e30
STEPS = 6


def rounds(segments):
    chips = segments // 2
    return [(max(m, 1), m + 1) for m in range(0, chips, 2)]


def taken(tiles, amount):
    lane = lax.broadcasted_iota(jnp.int32, tiles[0].shape, 1)
    turned = [pltpu.roll(tile, (LANES - amount) % LANES, 1) for tile in tiles]
    keep = lane < LANES - amount
    return [
        jnp.where(keep, turned[t], turned[min(t + 1, len(tiles) - 1)]) for t in range(len(tiles))
    ]


def kernel(
    rows,
    total,
    *refs,
):
    (near, far, across_far, conv, project, pair, floor, head, conv_bias, numbers) = refs[:10]
    (out, padded, sides, lefts, rights, floors, found) = refs[10:17]
    shifts = [numbers[0, place] for place in range(VIEWS)]
    flags = [numbers[0, VIEWS + place] for place in range(VIEWS)]
    dilations = [numbers[0, 2 * VIEWS + place] for place in range(2)]
    reach = rows + 2 * DMAX + 4
    span = -(-(BAND + rows + 2 * EDGE) // 16) * 16
    first = lax.axis_index("seg") * rows
    seq_rate = dilations[0]
    pair_rate = dilations[1]

    padded[0:EDGE, :] = jnp.zeros((EDGE, CHANNELS), jnp.float32)
    padded[EDGE + total :, :] = jnp.zeros(
        (padded.shape[0] - EDGE - total, CHANNELS), jnp.float32
    )
    me = lax.div(first, rows)
    pieces = [(near, 0, me)]
    for turn, masks in enumerate(rounds(total // rows)):
        even = lax.rem(me, 2) == 0
        ours = jnp.where(even, masks[0], masks[1])
        theirs = jnp.where(even, masks[1], masks[0])
        pieces.append((far, 2 * rows * turn, lax.bitwise_xor(me, 2 * ours)))
        pieces.append(
            (across_far, 2 * rows * turn, lax.bitwise_xor(lax.bitwise_xor(me, 1), 2 * theirs))
        )
    for ref, start, segment in pieces:
        for core in range(2):
            place = lax.bitwise_xor(segment, core) * rows
            padded[pl.ds(pl.multiple_of(EDGE + place, 8), rows), :] = ref[
                start + core * rows : start + (core + 1) * rows, :
            ].astype(jnp.float32)
    taps = [
        padded[pl.ds(first + DMAX + (tap - 1) * seq_rate, span), :] for tap in range(3)
    ]
    stacked = jnp.concatenate([tap.astype(jnp.bfloat16) for tap in taps], 1)
    mixed = jnp.dot(stacked, conv[...], preferred_element_type=jnp.float32)
    for flag in range(2):
        part = mixed[:, flag * CHANNELS : (flag + 1) * CHANNELS]
        feature = (taps[1] + jnp.maximum(part + conv_bias[...], 0.0)).astype(jnp.bfloat16)
        both = lax.dot_general(
            project[...], feature, (((1,), (1,)), ((), ())), preferred_element_type=jnp.float32
        )
        sides[flag, :, span:] = jnp.zeros((2 * PAIR_CH, sides.shape[2] - span), jnp.float32)
        sides[flag, :, 0:span] = both.astype(jnp.bfloat16).astype(jnp.float32)

    width = sides.shape[2]
    tiles = BAND // LANES
    lane = lax.broadcasted_iota(jnp.int32, (PAIR_CH, LANES), 1)

    def prepare(view):
        shift = shifts[view]
        flag = flags[view]
        both = sides[flag]
        cut = [both[:, t * LANES : (t + 1) * LANES] for t in range(width // LANES)]
        left = taken([c[:PAIR_CH] for c in cut[:2]], shift + HALO - DMAX)[0]
        place = first - DMAX + lane
        left = jnp.where((place >= 0) & (place < total), left, 0.0)
        turned = [left] + [pltpu.roll(left, LANES - by * pair_rate, 1) for by in (1, 2)]
        level = [
            pltpu.roll(value, (LANES + pair_rate - DMAX) % LANES, 1).astype(jnp.bfloat16)
            for value in turned
        ]
        spread = jnp.concatenate([value for value in level for _ in range(3)], 0)
        floors[view] = floor[...] - jnp.dot(
            pair[0:PAIR_CH, 0 : 9 * PAIR_CH], spread, preferred_element_type=jnp.float32
        )
        left = -left.astype(jnp.bfloat16)
        for row in range(reach):
            lefts[view, row] = jnp.broadcast_to(left[:, row : row + 1], (PAIR_CH, LANES))
        rights[view, STEPS] = jnp.full((PAIR_CH, width), OUT, jnp.bfloat16)
        for step in range(STEPS):
            offset = (step - 2) * pair_rate
            right = taken([c[PAIR_CH:] for c in cut], shift + HALO + offset)
            for t in range(width // LANES):
                rights[view, step, :, t * LANES : (t + 1) * LANES] = jnp.where(
                    first + offset + t * LANES + lane < total, right[t], OUT
                ).astype(jnp.bfloat16)

    for view in range(VIEWS):
        prepare(view)

    def group(number):
        block = lax.div(number, pair_rate)
        base = number + block * pair_rate
        sums = [[0.0] * tiles for _ in range(2)]
        offsets = [0.0, 0.0]
        wrapped = lane < base
        caps = [
            jnp.where(gone, OUT, -OUT).astype(jnp.bfloat16)
            for gone in (
                (lane >= base) & (lane < base + pair_rate),
                (lane >= base - pair_rate) & (lane < base),
                lane >= base - pair_rate + LANES,
            )
        ]
        for view in range(VIEWS):
            sides_of = [
                lefts[view, base + DMAX + (cell - 1) * pair_rate] for cell in range(4)
            ]
            kept = []
            for cell in range(4):
                place = first + base + (cell - 1) * pair_rate
                kept.append((place >= 0) & (place < total))
            lows = []
            for half in range(2):
                turned = pltpu.roll(floors[view], LANES - base - half * pair_rate, 1)
                lows.append(jnp.broadcast_to(turned[:, 0:1], (PAIR_CH, LANES)))
                for e in range(0, PAIR_CH, 8):
                    offsets[half] = offsets[half] + lows[half][e : e + 8] * head[e : e + 8, :]
            for wide in range(tiles // 2):
                chosen = (2 * wide, 2 * wide + 1)
                cells = []
                for cell in range(4):
                    for tap in range(3):
                        step = jnp.where(kept[cell], cell + tap, STEPS)
                        row = [
                            rights[view, step, :, t * LANES : (t + 1) * LANES] for t in chosen
                        ]
                        if wide == 0:
                            last = rights[view, step, :, tiles * LANES :]
                            row[0] = jnp.where(wrapped, last, row[0])
                        if wide == 0 and tap == 0:
                            row[0] = jnp.minimum(row[0], caps[0])
                        if wide == 0 and tap == 2:
                            row[0] = jnp.minimum(row[0], caps[1])
                        if wide == 1 and tap == 2:
                            row[1] = jnp.minimum(row[1], caps[2])
                        cells.append(
                            jnp.concatenate([jnp.maximum(r, sides_of[cell]) for r in row], 1)
                        )
                stack = jnp.concatenate(cells, 0)
                product = jnp.dot(pair[...], stack, preferred_element_type=jnp.float32)
                for half in range(2):
                    for t in chosen:
                        for e in range(0, PAIR_CH, 8):
                            part = product[
                                half * PAIR_CH + e : half * PAIR_CH + e + 8,
                                (t - chosen[0]) * LANES : (t - chosen[0] + 1) * LANES,
                            ]
                            sums[half][t] = (
                                sums[half][t]
                                + jnp.maximum(part, lows[half][e : e + 8]) * head[e : e + 8, :]
                            )
        sums = [[sums[half][t] - offsets[half] for t in range(tiles)] for half in range(2)]
        for half in range(2):
            found[base + half * pair_rate] = jnp.concatenate(sums[half], 1)

    def groups_of_two(number, carry):
        group(2 * number)
        group(2 * number + 1)
        return carry

    blocks = lax.div(rows + 2 * pair_rate - 1, 2 * pair_rate)
    lax.fori_loop(0, lax.div(blocks * pair_rate, 2), groups_of_two, 0)

    lane1 = lane[:1]
    for place in range(rows):
        block = lax.div(place, 2 * pair_rate)
        base = block * 2 * pair_rate + lax.rem(place - block * 2 * pair_rate, pair_rate)
        row = jnp.sum(found[place], axis=0, keepdims=True) * (1.0 / VIEWS)
        turned = [
            pltpu.roll(row[:, t * LANES : (t + 1) * LANES], lax.rem(LANES - base, LANES), 1)
            for t in range(tiles)
        ]
        out[place : place + 1, :] = jnp.concatenate(
            [
                jnp.where(lane1 < LANES - base, turned[t], turned[(t + 1) % tiles])
                for t in range(tiles)
            ],
            1,
        )


def weights_kernel(
    conv_weight,
    pair_left,
    pair_right,
    pair_weight,
    pair_bias,
    head,
    conv_bias,
    shifts,
    flags,
    dilations,
    conv,
    project,
    pair,
    floor,
    out_head,
    out_bias,
    out_numbers,
    wide,
):
    row = lax.broadcasted_iota(jnp.int32, (CHANNELS, CHANNELS), 0)
    column = lax.broadcasted_iota(jnp.int32, (CHANNELS, CHANNELS), 1)
    turn = (row + column == CHANNELS - 1).astype(jnp.float32).astype(jnp.bfloat16)
    for tap in range(3):
        here = slice(tap * CHANNELS, (tap + 1) * CHANNELS)
        there = slice((2 - tap) * CHANNELS, (3 - tap) * CHANNELS)
        conv[here, 0:CHANNELS] = conv_weight[here, :]
        conv[here, CHANNELS:] = jnp.dot(
            turn, conv_weight[there, :], preferred_element_type=jnp.float32
        ).astype(jnp.bfloat16)
    project[0:PAIR_CH, :] = pair_left[...]
    project[PAIR_CH:, :] = pair_right[...]
    taps = 9 * PAIR_CH
    wide[...] = jnp.zeros(wide.shape, jnp.float32)
    turned = pair_weight[...].astype(jnp.float32).T
    wide[0:PAIR_CH, 0:taps] = turned
    wide[PAIR_CH:, taps // 3 : taps // 3 + taps] = turned
    pair[...] = wide[...].astype(jnp.bfloat16)
    floor[...] = -jnp.broadcast_to(pair_bias[...], (LANES, PAIR_CH)).T
    out_bias[...] = conv_bias[...]
    out_numbers[:, 0:VIEWS] = shifts[...]
    out_numbers[:, VIEWS : 2 * VIEWS] = flags[...]
    out_numbers[:, 2 * VIEWS :] = dilations[...]
    out_head[...] = jnp.broadcast_to(head[...].astype(jnp.float32), (LANES, PAIR_CH)).T


def prepared(
    conv_weight,
    pair_left,
    pair_right,
    pair_weight,
    pair_bias,
    head,
    conv_bias,
    shifts,
    flags,
    dilations,
):
    whole = pl.BlockSpec(memory_space=pltpu.VMEM)
    made = [
        ((3 * CHANNELS, 2 * CHANNELS), jnp.bfloat16),
        ((2 * PAIR_CH, CHANNELS), jnp.bfloat16),
        ((2 * PAIR_CH, 12 * PAIR_CH), jnp.bfloat16),
        ((PAIR_CH, LANES), jnp.float32),
        ((PAIR_CH, LANES), jnp.float32),
        ((1, CHANNELS), jnp.float32),
        ((1, 2 * VIEWS + 2), jnp.int32),
    ]
    return pl.pallas_call(
        weights_kernel,
        out_shape=[pltpu.VMEM(*one) for one in made],
        in_specs=[whole] * 10,
        out_specs=[whole] * 7,
        scratch_shapes=[pltpu.VMEM((2 * PAIR_CH, 12 * PAIR_CH), jnp.float32)],
        cost_estimate=pl.CostEstimate(flops=10**9, bytes_accessed=10**6, transcendentals=0),
    )(
        conv_weight.reshape(3 * CHANNELS, CHANNELS),
        pair_left.T,
        pair_right.T,
        pair_weight.reshape(9 * PAIR_CH, PAIR_CH),
        pair_bias[None],
        head[None],
        conv_bias[None],
        shifts[None],
        flags[None],
        dilations[None],
    )


def main_call(rows, total, near, far, across_far, weights):
    span = -(-(BAND + rows + 2 * EDGE) // 16) * 16
    width = -(-span // LANES) * LANES
    whole = pl.BlockSpec(memory_space=pltpu.VMEM)
    return pl.pallas_call(
        functools.partial(kernel, rows, total),
        out_shape=jax.ShapeDtypeStruct((rows, BAND), jnp.float32),
        in_specs=[whole] * 10,
        out_specs=whole,
        scratch_shapes=[
            pltpu.VMEM((total + span + EDGE, CHANNELS), jnp.float32),
            pltpu.VMEM((2, 2 * PAIR_CH, width), jnp.float32),
            pltpu.VMEM((VIEWS, rows + 2 * DMAX + 4, PAIR_CH, LANES), jnp.bfloat16),
            pltpu.VMEM((VIEWS, STEPS + 1, PAIR_CH, width), jnp.bfloat16),
            pltpu.VMEM((VIEWS, PAIR_CH, LANES), jnp.float32),
            pltpu.VMEM((rows + 2 * DMAX, 8, BAND), jnp.float32),
        ],
        compiler_params=pltpu.CompilerParams(vmem_limit_bytes=40 << 20),
    )(near, far, across_far, *weights)


def per_device(
    bins,
    conv_weight,
    conv_bias,
    pair_left,
    pair_right,
    pair_weight,
    pair_bias,
    head,
    shifts,
    flags,
    dilations,
):
    rows = bins.shape[0]
    segments = lax.axis_size("seg")

    def exchanged(value, masks):
        route = [(i, i ^ masks[i % 2]) for i in range(segments)]
        return lax.ppermute(value, "seg", route)

    near = jnp.concatenate([bins, exchanged(bins, (1, 1))], 0)
    parts = [exchanged(near, (2 * even, 2 * odd)) for even, odd in rounds(segments)]
    weights = prepared(
        conv_weight,
        pair_left,
        pair_right,
        pair_weight,
        pair_bias,
        head,
        conv_bias,
        shifts,
        flags,
        dilations,
    )
    parts, weights = lax.optimization_barrier((parts, weights))
    far = jnp.concatenate(parts, 0)
    across_far = exchanged(far, (1, 1))
    return main_call(rows, rows * segments, near, far, across_far, weights)


def solution(mesh):
    placed = (P(("groups", "seg"), None), P(), P(), P(), P(), P(), P(), P(), P(), P(), P())
    return jax.shard_map(
        per_device,
        mesh=mesh,
        in_specs=placed,
        out_specs=P(("groups", "seg"), None),
        check_vma=False,
    )
```

time: 45.4 us -> 26.5 us (0.58)
  Pallas kernels: 26.8 us -> 14.9 us
  waiting for transfers between devices: 6.54 us -> 2.25 us
  local copies, waits for them, and re-layouts: 3.83 us -> 0.74 us
  starting transfers between devices: 7.52 us -> 8.35 us
    pallas_call x1 -> x2, Pallas kernels: 26.8 us -> 14.9 us  [the longest x1 13.6 us: main_call(): pl.pallas_call(functools.partial(kernel, rows, total), out_shape=jax.Shap...]
    ppermute x0 -> x6, starting transfers between devices: none -> 8.35 us  [exchanged(): return lax.ppermute(value, 'seg', route)]
    all_to_all x1 -> x0, starting transfers between devices: 7.52 us -> none  [per_device(): lax.all_to_all(jnp.broadcast_to(bins[None], (segments,) + bins.shape), 's...]
    all_to_all x1 -> x0, waiting for transfers between devices: 6.54 us -> none  [per_device(): lax.all_to_all(jnp.broadcast_to(bins[None], (segments,) + bins.shape), 's...]
    ppermute x0 -> x6, waiting for transfers between devices: none -> 2.25 us  [exchanged(): return lax.ppermute(value, 'seg', route)]
    broadcast_in_dim x3 -> x0, local copies, waits for them, and re-layouts: 1.49 us -> none  [the longest x1 1.35 us: per_device(): jnp.broadcast_to(bins[None], (segments,) + bins.shape)]
    unnamed x20 -> x4, local copies, waits for them, and re-layouts: 1.97 us -> 0.72 us
  transfers between devices with their start and end apart: 1 -> 6, of which waited for: 1 -> 3; matrix products, arithmetic and copies ran while one was open for 1% -> 3% of each run, Pallas kernels for 0% -> 5%
where the time goes in v2:
time: 26.5 us; the launch traced here: 26.2 us
  Pallas kernels  14.9 us (56%)
  starting transfers between devices  8.35 us (32%)
  waiting for transfers between devices  2.25 us (8%)
  local copies, waits for them, and re-layouts  0.74 us (3%)
    pallas_call x1, Pallas kernels, main_call(): pl.pallas_call(functools.partial(kernel, rows, total), out_shape=jax.Shap...  13.6 us
    ppermute x6, starting transfers between devices, exchanged(): return lax.ppermute(value, 'seg', route)  8.35 us
    ppermute x6, waiting for transfers between devices, exchanged(): return lax.ppermute(value, 'seg', route)  2.25 us
    pallas_call x1, Pallas kernels, prepared(): pl.pallas_call(weights_kernel, out_shape=[pltpu.VMEM(*one) for one in mad...  1.31 us
    unnamed x4, local copies, waits for them, and re-layouts  0.72 us
  transfers between devices with their start and end apart: 6, of which 3 were waited for; matrix products, arithmetic and copies ran while one was open for 3% of the time, Pallas kernels for 5%

profile of v2, /device:TPU:0, one launch (start us, length us, event | category | flops | bytes accessed | tf_op | source)
XLA Modules:
  0.0 26.2 jit_solution(4862791381348280675)
XLA Ops:
  0.0 0.5 %collective-permute-start = (bf16[32,128]{1,0:T(8,128)(2,1)}, bf16[32,128]{1,0:T(8,128)(2,1)S(1)}, u32[]{:S(2)}, u32[]{:S(2)}) collective-permute-start(bf16[32,128]{1,0:T(8,128)(2,1)} %param.11), channel_id=1, source_target_pairs={{0,1},{1,0},{2,3},{3,2},{4,5},{5,4},{6,7},{7,6},{8,9},{9,8},{10,11... | collective-permute-start | bytes 24584 | tf_op jit(solution)/shard_map/ppermute | solution.py:342
  0.5 0.7 %constant_dynamic-update-slice_fusion.1 = bf16[64,128]{1,0:T(8,128)(2,1)S(1)} fusion(bf16[32,128]{1,0:T(8,128)(2,1)} %param.11), kind=kLoop, calls=%fused_computation.1 | loop fusion | bytes 16384
  1.2 0.3 %collective-permute-done = bf16[32,128]{1,0:T(8,128)(2,1)S(1)} collective-permute-done((bf16[32,128]{1,0:T(8,128)(2,1)}, bf16[32,128]{1,0:T(8,128)(2,1)S(1)}, u32[]{:S(2)}, u32[]{:S(2)}) %collective-permute-start) | collective-permute-done | bytes 8224 | tf_op jit(solution)/shard_map/ppermute | solution.py:342
  1.5 4.9 %collective-permute-start.4 = (bf16[64,128]{1,0:T(8,128)(2,1)S(1)}, bf16[64,128]{1,0:T(8,128)(2,1)S(1)}, u32[]{:S(2)}, u32[]{:S(2)}) collective-permute-start(bf16[64,128]{1,0:T(8,128)(2,1)S(1)} %constant_dynamic-update-slice_fusion.refs_0_), channel_id=1, source_target_pairs={{0,12},{1,15},{2,14},{3,13},{4,8},{5,11},{6,10},{7,9},{8,4},{9,7},... | collective-permute-start | bytes 49160 | tf_op jit(solution)/shard_map/ppermute | solution.py:342
  6.4 0.0 collective-permute-start.3
  6.4 0.6 %collective-permute-start.2 = (bf16[64,128]{1,0:T(8,128)(2,1)S(1)}, bf16[64,128]{1,0:T(8,128)(2,1)S(1)}, u32[]{:S(2)}, u32[]{:S(2)}) collective-permute-start(bf16[64,128]{1,0:T(8,128)(2,1)S(1)} %constant_dynamic-update-slice_fusion.refs_0_), channel_id=1, source_target_pairs={{0,4},{1,7},{2,6},{3,5},{4,0},{5,3},{6,2},{7,1},{8,12},{9,15},{10,... | collective-permute-start | bytes 49160 | tf_op jit(solution)/shard_map/ppermute | solution.py:342
  7.0 1.7 %collective-permute-start.1 = (bf16[64,128]{1,0:T(8,128)(2,1)S(1)}, bf16[64,128]{1,0:T(8,128)(2,1)S(1)}, u32[]{:S(2)}, u32[]{:S(2)}) collective-permute-start(bf16[64,128]{1,0:T(8,128)(2,1)S(1)} %constant_dynamic-update-slice_fusion.refs_0_), channel_id=1, source_target_pairs={{0,2},{1,3},{2,0},{3,1},{4,6},{5,7},{6,4},{7,5},{8,10},{9,11},{10,... | collective-permute-start | bytes 49160 | tf_op jit(solution)/shard_map/ppermute | solution.py:342
  8.7 1.3 %shard_map.109 = (bf16[384,256]{1,0:T(8,128)(2,1)S(1)}, bf16[96,128]{1,0:T(8,128)(2,1)S(1)}, bf16[96,576]{1,0:T(8,128)(2,1)S(1)}, f32[48,128]{1,0:T(8,128)S(1)},...) custom-call(bf16[384,128]{1,0:T(8,128)(2,1)} %bitcast.11, bf16[48,128]{1,0:T(8,128)(2,1)} %bitcast.12, ...), custom_call_target="tpu_custom_call" | custom-call | flops 1000000000 | bytes 1000000 | tf_op jit(solution)/shard_map/pallas_call | solution.py:282
  10.1 0.0 collective-permute-done.4
  10.1 1.0 %collective-permute-done.3 = bf16[64,128]{1,0:T(8,128)(2,1)S(1)} collective-permute-done((bf16[64,128]{1,0:T(8,128)(2,1)S(1)}, bf16[64,128]{1,0:T(8,128)(2,1)S(1)}, u32[]{:S(2)}, u32[]{:S(2)}) %collective-permute-start.3) | collective-permute-done | bytes 16416 | tf_op jit(solution)/shard_map/ppermute | solution.py:342
  11.1 0.0 collective-permute-done.2
  11.1 0.0 collective-permute-done.1
  11.1 0.7 %collective-permute-start.5 = (bf16[256,128]{1,0:T(8,128)(2,1)S(1)}, bf16[256,128]{1,0:T(8,128)(2,1)S(1)}, u32[]{:S(2)}, u32[]{:S(2)}) collective-permute-start(bf16[256,128]{1,0:T(8,128)(2,1)S(1)} %constant_dynamic-update-slice_fusion.2.refs_1_), channel_id=1, source_target_pairs={{0,1},{1,0},{2,3},{3,2},{4,5},{5,4},{6,7},{7,6},{8,9},{9,8},{10,11... | collective-permute-start | bytes 196616 | tf_op jit(solution)/shard_map/ppermute | solution.py:342
  11.8 0.9 %collective-permute-done.5.refs_2_ = bf16[256,128]{1,0:T(8,128)(2,1)S(1)} collective-permute-done((bf16[256,128]{1,0:T(8,128)(2,1)S(1)}, bf16[256,128]{1,0:T(8,128)(2,1)S(1)}, u32[]{:S(2)}, u32[]{:S(2)}) %collective-permute-start.5) | collective-permute-done | bytes 65568 | tf_op jit(solution)/shard_map/ppermute | solution.py:342
  12.7 13.6 %shard_map.110 = f32[32,512]{1,0:T(8,128)} custom-call(bf16[64,128]{1,0:T(8,128)(2,1)S(1)} %constant_dynamic-update-slice_fusion.refs_0_, bf16[256,128]{1,0:T(8,128)(2,1)S(1)} %constant_dynamic-update-slice_fusion.2.refs_1_, bf16[256,128]{1,0:T(8,128)(2,1)S(1)} %collective-permute-done.5.refs_2_, bf16[384,256]{1,0:T(8,128)(2,1)S(1)} %get-tuple-element.34.refs_3_, ...), custom_call_target="tpu_custom_call" | custom-call | tf_op jit(solution)/shard_map/pallas_call | solution.py:307
  (5 shorter events, 0.0 us)
Async XLA Ops:
  0.0 1.5 %collective-permute-start = (bf16[32,128]{1,0:T(8,128)(2,1)}, bf16[32,128]{1,0:T(8,128)(2,1)S(1)}, u32[]{:S(2)}, u32[]{:S(2)}) collective-permute-start(bf16[32,128]{1,0:T(8,128)(2,1)} %param.11), channel_id=1, source_target_pairs={{0,1},{1,0},{2,3},{3,2},{4,5},{5,4},{6,7},{7,6},{8,9},{9,8},{10,11... | collective-permute-start | bytes 24584 | tf_op jit(solution)/shard_map/ppermute | solution.py:342
  1.5 8.6 %collective-permute-start.4 = (bf16[64,128]{1,0:T(8,128)(2,1)S(1)}, bf16[64,128]{1,0:T(8,128)(2,1)S(1)}, u32[]{:S(2)}, u32[]{:S(2)}) collective-permute-start(bf16[64,128]{1,0:T(8,128)(2,1)S(1)} %constant_dynamic-update-slice_fusion.refs_0_), channel_id=1, source_target_pairs={{0,12},{1,15},{2,14},{3,13},{4,8},{5,11},{6,10},{7,9},{8,4},{9,7},... | collective-permute-start | bytes 49160 | tf_op jit(solution)/shard_map/ppermute | solution.py:342
  6.4 4.6 %collective-permute-start.3 = (bf16[64,128]{1,0:T(8,128)(2,1)S(1)}, bf16[64,128]{1,0:T(8,128)(2,1)S(1)}, u32[]{:S(2)}, u32[]{:S(2)}) collective-permute-start(bf16[64,128]{1,0:T(8,128)(2,1)S(1)} %constant_dynamic-update-slice_fusion.refs_0_), channel_id=1, source_target_pairs={{0,8},{1,11},{2,10},{3,9},{4,12},{5,15},{6,14},{7,13},{8,0},{9,3},... | collective-permute-start | bytes 49160 | tf_op jit(solution)/shard_map/ppermute | solution.py:342
  6.4 4.6 %collective-permute-start.2 = (bf16[64,128]{1,0:T(8,128)(2,1)S(1)}, bf16[64,128]{1,0:T(8,128)(2,1)S(1)}, u32[]{:S(2)}, u32[]{:S(2)}) collective-permute-start(bf16[64,128]{1,0:T(8,128)(2,1)S(1)} %constant_dynamic-update-slice_fusion.refs_0_), channel_id=1, source_target_pairs={{0,4},{1,7},{2,6},{3,5},{4,0},{5,3},{6,2},{7,1},{8,12},{9,15},{10,... | collective-permute-start | bytes 49160 | tf_op jit(solution)/shard_map/ppermute | solution.py:342
  7.0 4.1 %collective-permute-start.1 = (bf16[64,128]{1,0:T(8,128)(2,1)S(1)}, bf16[64,128]{1,0:T(8,128)(2,1)S(1)}, u32[]{:S(2)}, u32[]{:S(2)}) collective-permute-start(bf16[64,128]{1,0:T(8,128)(2,1)S(1)} %constant_dynamic-update-slice_fusion.refs_0_), channel_id=1, source_target_pairs={{0,2},{1,3},{2,0},{3,1},{4,6},{5,7},{6,4},{7,5},{8,10},{9,11},{10,... | collective-permute-start | bytes 49160 | tf_op jit(solution)/shard_map/ppermute | solution.py:342
  11.1 1.6 %collective-permute-start.5 = (bf16[256,128]{1,0:T(8,128)(2,1)S(1)}, bf16[256,128]{1,0:T(8,128)(2,1)S(1)}, u32[]{:S(2)}, u32[]{:S(2)}) collective-permute-start(bf16[256,128]{1,0:T(8,128)(2,1)S(1)} %constant_dynamic-update-slice_fusion.2.refs_1_), channel_id=1, source_target_pairs={{0,1},{1,0},{2,3},{3,2},{4,5},{5,4},{6,7},{7,6},{8,9},{9,8},{10,11... | collective-permute-start | bytes 196616 | tf_op jit(solution)/shard_map/ppermute | solution.py:342

commit v3 on v2

--- a/solution.py
+++ b/solution.py
@@ -16,7 +16,10 @@
 EDGE = DMAX + HALO
 LANES = 128
 OUT = -1e30
-STEPS = 6
+PACK = 3
+SPREAD = 64
+CELLS = PACK + 2
+STEPS = PACK + 4
 
 
 def rounds(segments):
@@ -38,12 +41,12 @@
     total,
     *refs,
 ):
-    (near, far, across_far, conv, project, pair, floor, head, conv_bias, numbers) = refs[:10]
-    (out, padded, sides, lefts, rights, floors, found) = refs[10:17]
+    (near, far, across_far, conv, project, pair, floor, head, conv_bias, numbers, ones) = refs[:11]
+    (out, padded, sides, lefts, rights, floors, found) = refs[11:18]
     shifts = [numbers[0, place] for place in range(VIEWS)]
     flags = [numbers[0, VIEWS + place] for place in range(VIEWS)]
     dilations = [numbers[0, 2 * VIEWS + place] for place in range(2)]
-    reach = rows + 2 * DMAX + 4
+    reach = rows + 3 * DMAX
     span = -(-(BAND + rows + 2 * EDGE) // 16) * 16
     first = lax.axis_index("seg") * rows
     seq_rate = dilations[0]
@@ -80,8 +83,8 @@
         both = lax.dot_general(
             project[...], feature, (((1,), (1,)), ((), ())), preferred_element_type=jnp.float32
         )
-        sides[flag, :, span:] = jnp.zeros((2 * PAIR_CH, sides.shape[2] - span), jnp.float32)
-        sides[flag, :, 0:span] = both.astype(jnp.bfloat16).astype(jnp.float32)
+        sides[flag, :, span:] = jnp.zeros((2 * PAIR_CH, sides.shape[2] - span), jnp.bfloat16)
+        sides[flag, :, 0:span] = both.astype(jnp.bfloat16)
 
     width = sides.shape[2]
     tiles = BAND // LANES
@@ -94,83 +97,105 @@
         cut = [both[:, t * LANES : (t + 1) * LANES] for t in range(width // LANES)]
         left = taken([c[:PAIR_CH] for c in cut[:2]], shift + HALO - DMAX)[0]
         place = first - DMAX + lane
-        left = jnp.where((place >= 0) & (place < total), left, 0.0)
+        left = jnp.where((place >= 0) & (place < total), left, 0.0).astype(jnp.bfloat16)
         turned = [left] + [pltpu.roll(left, LANES - by * pair_rate, 1) for by in (1, 2)]
         level = [
-            pltpu.roll(value, (LANES + pair_rate - DMAX) % LANES, 1).astype(jnp.bfloat16)
+            pltpu.roll(value, (LANES + pair_rate - DMAX) % LANES, 1)
             for value in turned
         ]
         spread = jnp.concatenate([value for value in level for _ in range(3)], 0)
-        floors[view] = floor[...] - jnp.dot(
+        low = floor[...] - jnp.dot(
             pair[0:PAIR_CH, 0 : 9 * PAIR_CH], spread, preferred_element_type=jnp.float32
         )
-        left = -left.astype(jnp.bfloat16)
-        for row in range(reach):
-            lefts[view, row] = jnp.broadcast_to(left[:, row : row + 1], (PAIR_CH, LANES))
+        high = low.astype(jnp.bfloat16)
+        rest = (low - high.astype(jnp.float32)).astype(jnp.bfloat16)
+        lows_of.append(jnp.concatenate([high[:, 0:SPREAD], rest[:, 0:SPREAD]], 1))
+        rows_of.append(-left[:, 0:SPREAD])
         rights[view, STEPS] = jnp.full((PAIR_CH, width), OUT, jnp.bfloat16)
         for step in range(STEPS):
-            offset = (step - 2) * pair_rate
+            offset = (step - 3) * pair_rate
             right = taken([c[PAIR_CH:] for c in cut], shift + HALO + offset)
             for t in range(width // LANES):
                 rights[view, step, :, t * LANES : (t + 1) * LANES] = jnp.where(
                     first + offset + t * LANES + lane < total, right[t], OUT
                 ).astype(jnp.bfloat16)
 
+    rows_of = []
+    lows_of = []
     for view in range(VIEWS):
         prepare(view)
+    stacked = jnp.concatenate(rows_of, 0)
+    for row in range(0, reach, 4):
+        spread = jnp.dot(
+            stacked,
+            ones[0:SPREAD, row * LANES : (row + 4) * LANES],
+            preferred_element_type=jnp.float32
+        ).astype(jnp.bfloat16)
+        for view in range(VIEWS):
+            for which in range(4):
+                lefts[view, row + which] = spread[
+                    view * PAIR_CH : (view + 1) * PAIR_CH, which * LANES : (which + 1) * LANES
+                ]
+
+    stacked = jnp.concatenate(lows_of, 0)
+    for row in range(0, rows + 2 * DMAX, 4):
+        spread = jnp.dot(
+            stacked, ones[:, row * LANES : (row + 4) * LANES], preferred_element_type=jnp.float32
+        )
+        for view in range(VIEWS):
+            for which in range(4):
+                floors[view, row + which] = spread[
+                    view * PAIR_CH : (view + 1) * PAIR_CH, which * LANES : (which + 1) * LANES
+                ]
 
     def group(number):
         block = lax.div(number, pair_rate)
-        base = number + block * pair_rate
-        sums = [[0.0] * tiles for _ in range(2)]
-        offsets = [0.0, 0.0]
-        wrapped = lane < base
+        base = number + block * (PACK - 1) * pair_rate
+        sums = [[0.0] * tiles for _ in range(PACK)]
+        offsets = [0.0] * PACK
+        seam = base + pair_rate
+        wrapped = lane < seam
         caps = [
             jnp.where(gone, OUT, -OUT).astype(jnp.bfloat16)
             for gone in (
-                (lane >= base) & (lane < base + pair_rate),
-                (lane >= base - pair_rate) & (lane < base),
-                lane >= base - pair_rate + LANES,
+                (lane >= seam) & (lane < seam + pair_rate),
+                (lane >= base) & (lane < seam),
             )
         ]
         for view in range(VIEWS):
             sides_of = [
-                lefts[view, base + DMAX + (cell - 1) * pair_rate] for cell in range(4)
+                lefts[view, base + DMAX + (cell - 1) * pair_rate] for cell in range(CELLS)
             ]
-            kept = []
-            for cell in range(4):
-                place = first + base + (cell - 1) * pair_rate
-                kept.append((place >= 0) & (place < total))
+            above = first + base < pair_rate
             lows = []
-            for half in range(2):
-                turned = pltpu.roll(floors[view], LANES - base - half * pair_rate, 1)
-                lows.append(jnp.broadcast_to(turned[:, 0:1], (PAIR_CH, LANES)))
+            for half in range(PACK):
+                lows.append(floors[view, base + half * pair_rate])
                 for e in range(0, PAIR_CH, 8):
                     offsets[half] = offsets[half] + lows[half][e : e + 8] * head[e : e + 8, :]
             for wide in range(tiles // 2):
                 chosen = (2 * wide, 2 * wide + 1)
+                across = {}
+                for step in range(-3, STEPS):
+                    at = step if step >= 0 else jnp.where(above, STEPS, step + 3)
+                    row = [rights[view, at, :, t * LANES : (t + 1) * LANES] for t in chosen]
+                    if wide == 0:
+                        last = rights[view, at, :, tiles * LANES :]
+                        row[0] = jnp.where(wrapped, last, row[0])
+                    across[step] = row
                 cells = []
-                for cell in range(4):
+                for cell in range(CELLS):
                     for tap in range(3):
-                        step = jnp.where(kept[cell], cell + tap, STEPS)
-                        row = [
-                            rights[view, step, :, t * LANES : (t + 1) * LANES] for t in chosen
-                        ]
-                        if wide == 0:
-                            last = rights[view, step, :, tiles * LANES :]
-                            row[0] = jnp.where(wrapped, last, row[0])
+                        row = list(across[cell + tap if cell else tap - 3])
                         if wide == 0 and tap == 0:
                             row[0] = jnp.minimum(row[0], caps[0])
                         if wide == 0 and tap == 2:
                             row[0] = jnp.minimum(row[0], caps[1])
-                        if wide == 1 and tap == 2:
-                            row[1] = jnp.minimum(row[1], caps[2])
                         cells.append(
                             jnp.concatenate([jnp.maximum(r, sides_of[cell]) for r in row], 1)
                         )
                 stack = jnp.concatenate(cells, 0)
                 product = jnp.dot(pair[...], stack, preferred_element_type=jnp.float32)
-                for half in range(2):
+                for half in range(PACK):
                     for t in chosen:
                         for e in range(0, PAIR_CH, 8):
                             part = product[
@@ -181,8 +206,8 @@
                                 sums[half][t]
                                 + jnp.maximum(part, lows[half][e : e + 8]) * head[e : e + 8, :]
                             )
-        sums = [[sums[half][t] - offsets[half] for t in range(tiles)] for half in range(2)]
-        for half in range(2):
+        sums = [[sums[half][t] - offsets[half] for t in range(tiles)] for half in range(PACK)]
+        for half in range(PACK):
             found[base + half * pair_rate] = jnp.concatenate(sums[half], 1)
 
     def groups_of_two(number, carry):
@@ -190,14 +215,19 @@
         group(2 * number + 1)
         return carry
 
-    blocks = lax.div(rows + 2 * pair_rate - 1, 2 * pair_rate)
-    lax.fori_loop(0, lax.div(blocks * pair_rate, 2), groups_of_two, 0)
+    deep = PACK * pair_rate
+    groups = lax.div(rows + deep - 1, deep) * pair_rate
+    lax.fori_loop(0, lax.div(groups + 1, 2), groups_of_two, 0)
 
     lane1 = lane[:1]
+    summed = found[0:rows, 0, :]
+    for part in range(1, 8):
+        summed = summed + found[0:rows, part, :]
+    summed = summed * (1.0 / VIEWS)
     for place in range(rows):
-        block = lax.div(place, 2 * pair_rate)
-        base = block * 2 * pair_rate + lax.rem(place - block * 2 * pair_rate, pair_rate)
-        row = jnp.sum(found[place], axis=0, keepdims=True) * (1.0 / VIEWS)
+        block = lax.div(place, deep)
+        base = block * deep + lax.rem(place - block * deep, pair_rate) + pair_rate
+        row = summed[place : place + 1]
         turned = [
             pltpu.roll(row[:, t * LANES : (t + 1) * LANES], lax.rem(LANES - base, LANES), 1)
             for t in range(tiles)
@@ -229,6 +259,7 @@
     out_head,
     out_bias,
     out_numbers,
+    ones,
     wide,
 ):
     row = lax.broadcasted_iota(jnp.int32, (CHANNELS, CHANNELS), 0)
@@ -246,18 +277,23 @@
     taps = 9 * PAIR_CH
     wide[...] = jnp.zeros(wide.shape, jnp.float32)
     turned = pair_weight[...].astype(jnp.float32).T
-    wide[0:PAIR_CH, 0:taps] = turned
-    wide[PAIR_CH:, taps // 3 : taps // 3 + taps] = turned
+    for half in range(PACK):
+        start = half * (taps // 3)
+        wide[half * PAIR_CH : (half + 1) * PAIR_CH, start : start + taps] = turned
     pair[...] = wide[...].astype(jnp.bfloat16)
     floor[...] = -jnp.broadcast_to(pair_bias[...], (LANES, PAIR_CH)).T
     out_bias[...] = conv_bias[...]
     out_numbers[:, 0:VIEWS] = shifts[...]
     out_numbers[:, VIEWS : 2 * VIEWS] = flags[...]
     out_numbers[:, 2 * VIEWS :] = dilations[...]
+    row = lax.broadcasted_iota(jnp.int32, ones.shape, 0)
+    column = lax.broadcasted_iota(jnp.int32, ones.shape, 1)
+    ones[...] = (lax.rem(row, SPREAD) == lax.div(column, LANES)).astype(jnp.float32).astype(jnp.bfloat16)
     out_head[...] = jnp.broadcast_to(head[...].astype(jnp.float32), (LANES, PAIR_CH)).T
 
 
 def prepared(
+    reach,
     conv_weight,
     pair_left,
     pair_right,
@@ -273,18 +309,19 @@
     made = [
         ((3 * CHANNELS, 2 * CHANNELS), jnp.bfloat16),
         ((2 * PAIR_CH, CHANNELS), jnp.bfloat16),
-        ((2 * PAIR_CH, 12 * PAIR_CH), jnp.bfloat16),
+        ((PACK * PAIR_CH, 3 * CELLS * PAIR_CH), jnp.bfloat16),
         ((PAIR_CH, LANES), jnp.float32),
         ((PAIR_CH, LANES), jnp.float32),
         ((1, CHANNELS), jnp.float32),
         ((1, 2 * VIEWS + 2), jnp.int32),
+        ((2 * SPREAD, reach * LANES), jnp.bfloat16),
     ]
     return pl.pallas_call(
         weights_kernel,
         out_shape=[pltpu.VMEM(*one) for one in made],
         in_specs=[whole] * 10,
-        out_specs=[whole] * 7,
-        scratch_shapes=[pltpu.VMEM((2 * PAIR_CH, 12 * PAIR_CH), jnp.float32)],
+        out_specs=[whole] * 8,
+        scratch_shapes=[pltpu.VMEM((PACK * PAIR_CH, 3 * CELLS * PAIR_CH), jnp.float32)],
         cost_estimate=pl.CostEstimate(flops=10**9, bytes_accessed=10**6, transcendentals=0),
     )(
         conv_weight.reshape(3 * CHANNELS, CHANNELS),
@@ -307,14 +344,14 @@
     return pl.pallas_call(
         functools.partial(kernel, rows, total),
         out_shape=jax.ShapeDtypeStruct((rows, BAND), jnp.float32),
-        in_specs=[whole] * 10,
+        in_specs=[whole] * 11,
         out_specs=whole,
         scratch_shapes=[
             pltpu.VMEM((total + span + EDGE, CHANNELS), jnp.float32),
-            pltpu.VMEM((2, 2 * PAIR_CH, width), jnp.float32),
-            pltpu.VMEM((VIEWS, rows + 2 * DMAX + 4, PAIR_CH, LANES), jnp.bfloat16),
+            pltpu.VMEM((2, 2 * PAIR_CH, width), jnp.bfloat16),
+            pltpu.VMEM((VIEWS, rows + 3 * DMAX, PAIR_CH, LANES), jnp.bfloat16),
             pltpu.VMEM((VIEWS, STEPS + 1, PAIR_CH, width), jnp.bfloat16),
-            pltpu.VMEM((VIEWS, PAIR_CH, LANES), jnp.float32),
+            pltpu.VMEM((VIEWS, rows + 2 * DMAX, PAIR_CH, LANES), jnp.float32),
             pltpu.VMEM((rows + 2 * DMAX, 8, BAND), jnp.float32),
         ],
         compiler_params=pltpu.CompilerParams(vmem_limit_bytes=40 << 20),
@@ -344,6 +381,7 @@
     near = jnp.concatenate([bins, exchanged(bins, (1, 1))], 0)
     parts = [exchanged(near, (2 * even, 2 * odd)) for even, odd in rounds(segments)]
     weights = prepared(
+        rows + 3 * DMAX,
         conv_weight,
         pair_left,
         pair_right,

time: 26.5 us -> 25.3 us (0.955)
  Pallas kernels: 14.9 us -> 13.8 us
    pallas_call x1, Pallas kernels: 13.6 us -> 12.4 us  [main_call(): pl.pallas_call(functools.partial(kernel, rows, total), out_shape=jax.Shap...]
  transfers between devices with their start and end apart: 6 -> 6, of which waited for: 3 -> 3; matrix products, arithmetic and copies ran while one was open for 3% -> 3% of each run, Pallas kernels for 5% -> 6%
where the time goes in v3:
time: 25.3 us; the launch traced here: 25.1 us
  Pallas kernels  13.8 us (55%)
  starting transfers between devices  8.35 us (33%)
  waiting for transfers between devices  2.17 us (9%)
  local copies, waits for them, and re-layouts  0.74 us (3%)
    pallas_call x1, Pallas kernels, main_call(): pl.pallas_call(functools.partial(kernel, rows, total), out_shape=jax.Shap...  12.4 us
    ppermute x6, starting transfers between devices, exchanged(): return lax.ppermute(value, 'seg', route)  8.35 us
    ppermute x6, waiting for transfers between devices, exchanged(): return lax.ppermute(value, 'seg', route)  2.17 us
    pallas_call x1, Pallas kernels, prepared(): pl.pallas_call(weights_kernel, out_shape=[pltpu.VMEM(*one) for one in mad...  1.39 us
    unnamed x4, local copies, waits for them, and re-layouts  0.72 us
  transfers between devices with their start and end apart: 6, of which 3 were waited for; matrix products, arithmetic and copies ran while one was open for 3% of the time, Pallas kernels for 6%

profile of v3, /device:TPU:0, one launch (start us, length us, event | category | flops | bytes accessed | tf_op | source)
XLA Modules:
  0.0 25.1 jit_solution(10441512301163601466)
XLA Ops:
  0.0 0.5 %collective-permute-start = (bf16[32,128]{1,0:T(8,128)(2,1)}, bf16[32,128]{1,0:T(8,128)(2,1)S(1)}, u32[]{:S(2)}, u32[]{:S(2)}) collective-permute-start(bf16[32,128]{1,0:T(8,128)(2,1)} %param.11), channel_id=1, source_target_pairs={{0,1},{1,0},{2,3},{3,2},{4,5},{5,4},{6,7},{7,6},{8,9},{9,8},{10,11... | collective-permute-start | bytes 24584 | tf_op jit(solution)/shard_map/ppermute | solution.py:379
  0.5 0.7 %constant_dynamic-update-slice_fusion.1 = bf16[64,128]{1,0:T(8,128)(2,1)S(1)} fusion(bf16[32,128]{1,0:T(8,128)(2,1)} %param.11), kind=kLoop, calls=%fused_computation.1 | loop fusion | bytes 16384
  1.2 0.3 %collective-permute-done = bf16[32,128]{1,0:T(8,128)(2,1)S(1)} collective-permute-done((bf16[32,128]{1,0:T(8,128)(2,1)}, bf16[32,128]{1,0:T(8,128)(2,1)S(1)}, u32[]{:S(2)}, u32[]{:S(2)}) %collective-permute-start) | collective-permute-done | bytes 8224 | tf_op jit(solution)/shard_map/ppermute | solution.py:379
  1.5 4.9 %collective-permute-start.4 = (bf16[64,128]{1,0:T(8,128)(2,1)S(1)}, bf16[64,128]{1,0:T(8,128)(2,1)S(1)}, u32[]{:S(2)}, u32[]{:S(2)}) collective-permute-start(bf16[64,128]{1,0:T(8,128)(2,1)S(1)} %constant_dynamic-update-slice_fusion.refs_0_), channel_id=1, source_target_pairs={{0,12},{1,15},{2,14},{3,13},{4,8},{5,11},{6,10},{7,9},{8,4},{9,7},... | collective-permute-start | bytes 49160 | tf_op jit(solution)/shard_map/ppermute | solution.py:379
  6.4 0.0 collective-permute-start.3
  6.4 0.6 %collective-permute-start.2 = (bf16[64,128]{1,0:T(8,128)(2,1)S(1)}, bf16[64,128]{1,0:T(8,128)(2,1)S(1)}, u32[]{:S(2)}, u32[]{:S(2)}) collective-permute-start(bf16[64,128]{1,0:T(8,128)(2,1)S(1)} %constant_dynamic-update-slice_fusion.refs_0_), channel_id=1, source_target_pairs={{0,4},{1,7},{2,6},{3,5},{4,0},{5,3},{6,2},{7,1},{8,12},{9,15},{10,... | collective-permute-start | bytes 49160 | tf_op jit(solution)/shard_map/ppermute | solution.py:379
  7.0 1.7 %collective-permute-start.1 = (bf16[64,128]{1,0:T(8,128)(2,1)S(1)}, bf16[64,128]{1,0:T(8,128)(2,1)S(1)}, u32[]{:S(2)}, u32[]{:S(2)}) collective-permute-start(bf16[64,128]{1,0:T(8,128)(2,1)S(1)} %constant_dynamic-update-slice_fusion.refs_0_), channel_id=1, source_target_pairs={{0,2},{1,3},{2,0},{3,1},{4,6},{5,7},{6,4},{7,5},{8,10},{9,11},{10,... | collective-permute-start | bytes 49160 | tf_op jit(solution)/shard_map/ppermute | solution.py:379
  8.7 1.4 %shard_map.109 = (bf16[384,256]{1,0:T(8,128)(2,1)S(1)}, bf16[96,128]{1,0:T(8,128)(2,1)S(1)}, bf16[144,720]{1,0:T(8,128)(2,1)S(1)}, f32[48,128]{1,0:T(8,128)S(1)}...) custom-call(bf16[384,128]{1,0:T(8,128)(2,1)} %bitcast.11, ...), custom_call_target="tpu_custom_call" | custom-call | flops 1000000000 | bytes 1000000 | tf_op jit(solution)/shard_map/pallas_call | solution.py:319
  10.1 0.0 collective-permute-done.4
  10.2 0.9 %collective-permute-done.3 = bf16[64,128]{1,0:T(8,128)(2,1)S(1)} collective-permute-done((bf16[64,128]{1,0:T(8,128)(2,1)S(1)}, bf16[64,128]{1,0:T(8,128)(2,1)S(1)}, u32[]{:S(2)}, u32[]{:S(2)}) %collective-permute-start.3) | collective-permute-done | bytes 16416 | tf_op jit(solution)/shard_map/ppermute | solution.py:379
  11.1 0.0 collective-permute-done.2
  11.1 0.0 collective-permute-done.1
  11.1 0.7 %collective-permute-start.5 = (bf16[256,128]{1,0:T(8,128)(2,1)S(1)}, bf16[256,128]{1,0:T(8,128)(2,1)S(1)}, u32[]{:S(2)}, u32[]{:S(2)}) collective-permute-start(bf16[256,128]{1,0:T(8,128)(2,1)S(1)} %constant_dynamic-update-slice_fusion.2.refs_1_), channel_id=1, source_target_pairs={{0,1},{1,0},{2,3},{3,2},{4,5},{5,4},{6,7},{7,6},{8,9},{9,8},{10,11... | collective-permute-start | bytes 196616 | tf_op jit(solution)/shard_map/ppermute | solution.py:379
  11.8 0.9 %collective-permute-done.5.refs_2_ = bf16[256,128]{1,0:T(8,128)(2,1)S(1)} collective-permute-done((bf16[256,128]{1,0:T(8,128)(2,1)S(1)}, bf16[256,128]{1,0:T(8,128)(2,1)S(1)}, u32[]{:S(2)}, u32[]{:S(2)}) %collective-permute-start.5) | collective-permute-done | bytes 65568 | tf_op jit(solution)/shard_map/ppermute | solution.py:379
  12.7 12.4 %shard_map.110 = f32[32,512]{1,0:T(8,128)} custom-call(bf16[64,128]{1,0:T(8,128)(2,1)S(1)} %constant_dynamic-update-slice_fusion.refs_0_, bf16[256,128]{1,0:T(8,128)(2,1)S(1)} %constant_dynamic-update-slice_fusion.2.refs_1_, bf16[256,128]{1,0:T(8,128)(2,1)S(1)} %collective-permute-done.5.refs_2_, bf16[384,256]{1,0:T(8,128)(2,1)S(1)} %get-tuple-element.37.refs_3_, ...), custom_call_target="tpu_custom_call" | custom-call | tf_op jit(solution)/shard_map/pallas_call | solution.py:344
  (5 shorter events, 0.0 us)
Async XLA Ops:
  0.0 1.5 %collective-permute-start = (bf16[32,128]{1,0:T(8,128)(2,1)}, bf16[32,128]{1,0:T(8,128)(2,1)S(1)}, u32[]{:S(2)}, u32[]{:S(2)}) collective-permute-start(bf16[32,128]{1,0:T(8,128)(2,1)} %param.11), channel_id=1, source_target_pairs={{0,1},{1,0},{2,3},{3,2},{4,5},{5,4},{6,7},{7,6},{8,9},{9,8},{10,11... | collective-permute-start | bytes 24584 | tf_op jit(solution)/shard_map/ppermute | solution.py:379
  1.5 8.7 %collective-permute-start.4 = (bf16[64,128]{1,0:T(8,128)(2,1)S(1)}, bf16[64,128]{1,0:T(8,128)(2,1)S(1)}, u32[]{:S(2)}, u32[]{:S(2)}) collective-permute-start(bf16[64,128]{1,0:T(8,128)(2,1)S(1)} %constant_dynamic-update-slice_fusion.refs_0_), channel_id=1, source_target_pairs={{0,12},{1,15},{2,14},{3,13},{4,8},{5,11},{6,10},{7,9},{8,4},{9,7},... | collective-permute-start | bytes 49160 | tf_op jit(solution)/shard_map/ppermute | solution.py:379
  6.4 4.6 %collective-permute-start.3 = (bf16[64,128]{1,0:T(8,128)(2,1)S(1)}, bf16[64,128]{1,0:T(8,128)(2,1)S(1)}, u32[]{:S(2)}, u32[]{:S(2)}) collective-permute-start(bf16[64,128]{1,0:T(8,128)(2,1)S(1)} %constant_dynamic-update-slice_fusion.refs_0_), channel_id=1, source_target_pairs={{0,8},{1,11},{2,10},{3,9},{4,12},{5,15},{6,14},{7,13},{8,0},{9,3},... | collective-permute-start | bytes 49160 | tf_op jit(solution)/shard_map/ppermute | solution.py:379
  6.4 4.6 %collective-permute-start.2 = (bf16[64,128]{1,0:T(8,128)(2,1)S(1)}, bf16[64,128]{1,0:T(8,128)(2,1)S(1)}, u32[]{:S(2)}, u32[]{:S(2)}) collective-permute-start(bf16[64,128]{1,0:T(8,128)(2,1)S(1)} %constant_dynamic-update-slice_fusion.refs_0_), channel_id=1, source_target_pairs={{0,4},{1,7},{2,6},{3,5},{4,0},{5,3},{6,2},{7,1},{8,12},{9,15},{10,... | collective-permute-start | bytes 49160 | tf_op jit(solution)/shard_map/ppermute | solution.py:379
  7.0 4.1 %collective-permute-start.1 = (bf16[64,128]{1,0:T(8,128)(2,1)S(1)}, bf16[64,128]{1,0:T(8,128)(2,1)S(1)}, u32[]{:S(2)}, u32[]{:S(2)}) collective-permute-start(bf16[64,128]{1,0:T(8,128)(2,1)S(1)} %constant_dynamic-update-slice_fusion.refs_0_), channel_id=1, source_target_pairs={{0,2},{1,3},{2,0},{3,1},{4,6},{5,7},{6,4},{7,5},{8,10},{9,11},{10,... | collective-permute-start | bytes 49160 | tf_op jit(solution)/shard_map/ppermute | solution.py:379
  11.1 1.6 %collective-permute-start.5 = (bf16[256,128]{1,0:T(8,128)(2,1)S(1)}, bf16[256,128]{1,0:T(8,128)(2,1)S(1)}, u32[]{:S(2)}, u32[]{:S(2)}) collective-permute-start(bf16[256,128]{1,0:T(8,128)(2,1)S(1)} %constant_dynamic-update-slice_fusion.2.refs_1_), channel_id=1, source_target_pairs={{0,1},{1,0},{2,3},{3,2},{4,5},{5,4},{6,7},{7,6},{8,9},{9,8},{10,11... | collective-permute-start | bytes 196616 | tf_op jit(solution)/shard_map/ppermute | solution.py:379

commit v4 on v3

--- a/solution.py
+++ b/solution.py
@@ -17,6 +17,7 @@
 LANES = 128
 OUT = -1e30
 PACK = 3
+TOGETHER = 4
 SPREAD = 64
 CELLS = PACK + 2
 STEPS = PACK + 4
@@ -210,14 +211,14 @@
         for half in range(PACK):
             found[base + half * pair_rate] = jnp.concatenate(sums[half], 1)
 
-    def groups_of_two(number, carry):
-        group(2 * number)
-        group(2 * number + 1)
+    def some_groups(number, carry):
+        for which in range(TOGETHER):
+            group(TOGETHER * number + which)
         return carry
 
     deep = PACK * pair_rate
     groups = lax.div(rows + deep - 1, deep) * pair_rate
-    lax.fori_loop(0, lax.div(groups + 1, 2), groups_of_two, 0)
+    lax.fori_loop(0, lax.div(groups + TOGETHER - 1, TOGETHER), some_groups, 0)
 
     lane1 = lane[:1]
     summed = found[0:rows, 0, :]

time: 25.3 us -> 24.6 us (0.972)
  Pallas kernels: 13.8 us -> 13.1 us
    pallas_call x1, Pallas kernels: 12.4 us -> 11.7 us  [main_call(): pl.pallas_call(functools.partial(kernel, rows, total), out_shape=jax.Shap...]
where the time goes in v4:
time: 24.6 us; the launch traced here: 24.4 us
  Pallas kernels  13.1 us (53%)
  starting transfers between devices  8.35 us (34%)
  waiting for transfers between devices  2.17 us (9%)
  local copies, waits for them, and re-layouts  0.74 us (3%)
    pallas_call x1, Pallas kernels, main_call(): pl.pallas_call(functools.partial(kernel, rows, total), out_shape=jax.Shap...  11.7 us
    ppermute x6, starting transfers between devices, exchanged(): return lax.ppermute(value, 'seg', route)  8.35 us
    ppermute x6, waiting for transfers between devices, exchanged(): return lax.ppermute(value, 'seg', route)  2.17 us
    pallas_call x1, Pallas kernels, prepared(): pl.pallas_call(weights_kernel, out_shape=[pltpu.VMEM(*one) for one in mad...  1.39 us
    unnamed x4, local copies, waits for them, and re-layouts  0.72 us
  transfers between devices with their start and end apart: 6, of which 3 were waited for; matrix products, arithmetic and copies ran while one was open for 3% of the time, Pallas kernels for 6%

profile of v4, /device:TPU:0, one launch (start us, length us, event | category | flops | bytes accessed | tf_op | source)
XLA Modules:
  0.0 24.4 jit_solution(11052574543348494156)
XLA Ops:
  0.0 0.5 %collective-permute-start = (bf16[32,128]{1,0:T(8,128)(2,1)}, bf16[32,128]{1,0:T(8,128)(2,1)S(1)}, u32[]{:S(2)}, u32[]{:S(2)}) collective-permute-start(bf16[32,128]{1,0:T(8,128)(2,1)} %param.11), channel_id=1, source_target_pairs={{0,1},{1,0},{2,3},{3,2},{4,5},{5,4},{6,7},{7,6},{8,9},{9,8},{10,11... | collective-permute-start | bytes 24584 | tf_op jit(solution)/shard_map/ppermute | solution.py:380
  0.5 0.7 %constant_dynamic-update-slice_fusion.1 = bf16[64,128]{1,0:T(8,128)(2,1)S(1)} fusion(bf16[32,128]{1,0:T(8,128)(2,1)} %param.11), kind=kLoop, calls=%fused_computation.1 | loop fusion | bytes 16384
  1.2 0.3 %collective-permute-done = bf16[32,128]{1,0:T(8,128)(2,1)S(1)} collective-permute-done((bf16[32,128]{1,0:T(8,128)(2,1)}, bf16[32,128]{1,0:T(8,128)(2,1)S(1)}, u32[]{:S(2)}, u32[]{:S(2)}) %collective-permute-start) | collective-permute-done | bytes 8224 | tf_op jit(solution)/shard_map/ppermute | solution.py:380
  1.5 4.9 %collective-permute-start.4 = (bf16[64,128]{1,0:T(8,128)(2,1)S(1)}, bf16[64,128]{1,0:T(8,128)(2,1)S(1)}, u32[]{:S(2)}, u32[]{:S(2)}) collective-permute-start(bf16[64,128]{1,0:T(8,128)(2,1)S(1)} %constant_dynamic-update-slice_fusion.refs_0_), channel_id=1, source_target_pairs={{0,12},{1,15},{2,14},{3,13},{4,8},{5,11},{6,10},{7,9},{8,4},{9,7},... | collective-permute-start | bytes 49160 | tf_op jit(solution)/shard_map/ppermute | solution.py:380
  6.4 0.0 collective-permute-start.3
  6.4 0.6 %collective-permute-start.2 = (bf16[64,128]{1,0:T(8,128)(2,1)S(1)}, bf16[64,128]{1,0:T(8,128)(2,1)S(1)}, u32[]{:S(2)}, u32[]{:S(2)}) collective-permute-start(bf16[64,128]{1,0:T(8,128)(2,1)S(1)} %constant_dynamic-update-slice_fusion.refs_0_), channel_id=1, source_target_pairs={{0,4},{1,7},{2,6},{3,5},{4,0},{5,3},{6,2},{7,1},{8,12},{9,15},{10,... | collective-permute-start | bytes 49160 | tf_op jit(solution)/shard_map/ppermute | solution.py:380
  7.0 1.7 %collective-permute-start.1 = (bf16[64,128]{1,0:T(8,128)(2,1)S(1)}, bf16[64,128]{1,0:T(8,128)(2,1)S(1)}, u32[]{:S(2)}, u32[]{:S(2)}) collective-permute-start(bf16[64,128]{1,0:T(8,128)(2,1)S(1)} %constant_dynamic-update-slice_fusion.refs_0_), channel_id=1, source_target_pairs={{0,2},{1,3},{2,0},{3,1},{4,6},{5,7},{6,4},{7,5},{8,10},{9,11},{10,... | collective-permute-start | bytes 49160 | tf_op jit(solution)/shard_map/ppermute | solution.py:380
  8.7 1.4 %shard_map.109 = (bf16[384,256]{1,0:T(8,128)(2,1)S(1)}, bf16[96,128]{1,0:T(8,128)(2,1)S(1)}, bf16[144,720]{1,0:T(8,128)(2,1)S(1)}, f32[48,128]{1,0:T(8,128)S(1)}...) custom-call(bf16[384,128]{1,0:T(8,128)(2,1)} %bitcast.11, ...), custom_call_target="tpu_custom_call" | custom-call | flops 1000000000 | bytes 1000000 | tf_op jit(solution)/shard_map/pallas_call | solution.py:320
  10.1 0.0 collective-permute-done.4
  10.2 0.9 %collective-permute-done.3 = bf16[64,128]{1,0:T(8,128)(2,1)S(1)} collective-permute-done((bf16[64,128]{1,0:T(8,128)(2,1)S(1)}, bf16[64,128]{1,0:T(8,128)(2,1)S(1)}, u32[]{:S(2)}, u32[]{:S(2)}) %collective-permute-start.3) | collective-permute-done | bytes 16416 | tf_op jit(solution)/shard_map/ppermute | solution.py:380
  11.1 0.0 collective-permute-done.2
  11.1 0.0 collective-permute-done.1
  11.1 0.7 %collective-permute-start.5 = (bf16[256,128]{1,0:T(8,128)(2,1)S(1)}, bf16[256,128]{1,0:T(8,128)(2,1)S(1)}, u32[]{:S(2)}, u32[]{:S(2)}) collective-permute-start(bf16[256,128]{1,0:T(8,128)(2,1)S(1)} %constant_dynamic-update-slice_fusion.2.refs_1_), channel_id=1, source_target_pairs={{0,1},{1,0},{2,3},{3,2},{4,5},{5,4},{6,7},{7,6},{8,9},{9,8},{10,11... | collective-permute-start | bytes 196616 | tf_op jit(solution)/shard_map/ppermute | solution.py:380
  11.8 0.9 %collective-permute-done.5.refs_2_ = bf16[256,128]{1,0:T(8,128)(2,1)S(1)} collective-permute-done((bf16[256,128]{1,0:T(8,128)(2,1)S(1)}, bf16[256,128]{1,0:T(8,128)(2,1)S(1)}, u32[]{:S(2)}, u32[]{:S(2)}) %collective-permute-start.5) | collective-permute-done | bytes 65568 | tf_op jit(solution)/shard_map/ppermute | solution.py:380
  12.7 11.7 %shard_map.110 = f32[32,512]{1,0:T(8,128)} custom-call(bf16[64,128]{1,0:T(8,128)(2,1)S(1)} %constant_dynamic-update-slice_fusion.refs_0_, bf16[256,128]{1,0:T(8,128)(2,1)S(1)} %constant_dynamic-update-slice_fusion.2.refs_1_, bf16[256,128]{1,0:T(8,128)(2,1)S(1)} %collective-permute-done.5.refs_2_, bf16[384,256]{1,0:T(8,128)(2,1)S(1)} %get-tuple-element.37.refs_3_, ...), custom_call_target="tpu_custom_call" | custom-call | tf_op jit(solution)/shard_map/pallas_call | solution.py:345
  (5 shorter events, 0.0 us)
Async XLA Ops:
  0.0 1.5 %collective-permute-start = (bf16[32,128]{1,0:T(8,128)(2,1)}, bf16[32,128]{1,0:T(8,128)(2,1)S(1)}, u32[]{:S(2)}, u32[]{:S(2)}) collective-permute-start(bf16[32,128]{1,0:T(8,128)(2,1)} %param.11), channel_id=1, source_target_pairs={{0,1},{1,0},{2,3},{3,2},{4,5},{5,4},{6,7},{7,6},{8,9},{9,8},{10,11... | collective-permute-start | bytes 24584 | tf_op jit(solution)/shard_map/ppermute | solution.py:380
  1.5 8.7 %collective-permute-start.4 = (bf16[64,128]{1,0:T(8,128)(2,1)S(1)}, bf16[64,128]{1,0:T(8,128)(2,1)S(1)}, u32[]{:S(2)}, u32[]{:S(2)}) collective-permute-start(bf16[64,128]{1,0:T(8,128)(2,1)S(1)} %constant_dynamic-update-slice_fusion.refs_0_), channel_id=1, source_target_pairs={{0,12},{1,15},{2,14},{3,13},{4,8},{5,11},{6,10},{7,9},{8,4},{9,7},... | collective-permute-start | bytes 49160 | tf_op jit(solution)/shard_map/ppermute | solution.py:380
  6.4 4.6 %collective-permute-start.3 = (bf16[64,128]{1,0:T(8,128)(2,1)S(1)}, bf16[64,128]{1,0:T(8,128)(2,1)S(1)}, u32[]{:S(2)}, u32[]{:S(2)}) collective-permute-start(bf16[64,128]{1,0:T(8,128)(2,1)S(1)} %constant_dynamic-update-slice_fusion.refs_0_), channel_id=1, source_target_pairs={{0,8},{1,11},{2,10},{3,9},{4,12},{5,15},{6,14},{7,13},{8,0},{9,3},... | collective-permute-start | bytes 49160 | tf_op jit(solution)/shard_map/ppermute | solution.py:380
  6.4 4.6 %collective-permute-start.2 = (bf16[64,128]{1,0:T(8,128)(2,1)S(1)}, bf16[64,128]{1,0:T(8,128)(2,1)S(1)}, u32[]{:S(2)}, u32[]{:S(2)}) collective-permute-start(bf16[64,128]{1,0:T(8,128)(2,1)S(1)} %constant_dynamic-update-slice_fusion.refs_0_), channel_id=1, source_target_pairs={{0,4},{1,7},{2,6},{3,5},{4,0},{5,3},{6,2},{7,1},{8,12},{9,15},{10,... | collective-permute-start | bytes 49160 | tf_op jit(solution)/shard_map/ppermute | solution.py:380
  7.0 4.1 %collective-permute-start.1 = (bf16[64,128]{1,0:T(8,128)(2,1)S(1)}, bf16[64,128]{1,0:T(8,128)(2,1)S(1)}, u32[]{:S(2)}, u32[]{:S(2)}) collective-permute-start(bf16[64,128]{1,0:T(8,128)(2,1)S(1)} %constant_dynamic-update-slice_fusion.refs_0_), channel_id=1, source_target_pairs={{0,2},{1,3},{2,0},{3,1},{4,6},{5,7},{6,4},{7,5},{8,10},{9,11},{10,... | collective-permute-start | bytes 49160 | tf_op jit(solution)/shard_map/ppermute | solution.py:380
  11.1 1.6 %collective-permute-start.5 = (bf16[256,128]{1,0:T(8,128)(2,1)S(1)}, bf16[256,128]{1,0:T(8,128)(2,1)S(1)}, u32[]{:S(2)}, u32[]{:S(2)}) collective-permute-start(bf16[256,128]{1,0:T(8,128)(2,1)S(1)} %constant_dynamic-update-slice_fusion.2.refs_1_), channel_id=1, source_target_pairs={{0,1},{1,0},{2,3},{3,2},{4,5},{5,4},{6,7},{7,6},{8,9},{9,8},{10,11... | collective-permute-start | bytes 196616 | tf_op jit(solution)/shard_map/ppermute | solution.py:380
